TPU v7x, 32 devices: a whole 2x2x4 slice. The times are simulated.
32 devices in a mesh: kv: 2 (over x), qh: 2 (over y), seq: 8 (over z, core).
Axes of the slice: x: 2, y: 2, z: 4, core: 2. Of those that a mesh axis runs over, the one named last changes fastest.
Arguments:
- tokens: bfloat16 [8, 1024, 1536], P(('kv', 'qh'), 'seq'), may hold values from -6 to 6
- attn_gain: bfloat16 [1536], replicated, may hold values from 0.5 to 1.5
- query_weight: bfloat16 [1536, 1536], P(None, ('kv', 'qh')), may hold values from -0.15625 to 0.15625
- query_bias: bfloat16 [1536], P(('kv', 'qh')), may hold values from -3 to 3
- key_matrix: bfloat16 [1536, 256], P(None, 'kv'), may hold values from -0.15625 to 0.15625
- key_offset_bias: bfloat16 [256], P('kv'), may hold values from -3 to 3
- value_matrix: bfloat16 [1536, 256], P(None, 'kv'), may hold values from -0.15625 to 0.15625
- value_offset_bias: bfloat16 [256], P('kv'), may hold values from -0.29882812 to 0.29882812
- out_weight: bfloat16 [1536, 1536], P(('kv', 'qh')), may hold values from -1.25 to 1.25
- mlp_gain: bfloat16 [1536], replicated, may hold values from 0.5 to 1.5
- gate_weight: bfloat16 [1536, 8960], P(None, ('kv', 'qh')), may hold values from -0.15625 to 0.15625
- up_weight: bfloat16 [1536, 8960], P(None, ('kv', 'qh')), may hold values from -0.15625 to 0.15625
- down_weight: bfloat16 [8960, 1536], P(('kv', 'qh')), may hold values from -0.0625 to 0.0625
- segment_ids: int32 [8, 1024], replicated, may hold values from 0 to 4, as said below
- position_ids: int32 [8, 1024], P(None, 'seq'), may hold values from 0 to 1023, as said below
- cotangent: bfloat16 [8, 1024, 1536], P(('kv', 'qh'), 'seq'), may hold values from -6 to 6
Outputs:
- output: bfloat16 [8, 1024, 1536], P(('kv', 'qh'), 'seq')
- tokens_grad: float32 [8, 1024, 1536], P(('kv', 'qh'), 'seq')
- attn_gain_grad: float32 [1536], replicated
- query_weight_grad: float32 [1536, 1536], P('seq', ('kv', 'qh'))
- query_bias_grad: float32 [1536], replicated
- key_weight_grad: float32 [1536, 256], replicated
- key_bias_grad: float32 [256], replicated
- value_weight_grad: float32 [1536, 256], replicated
- value_bias_grad: float32 [256], replicated
- out_weight_grad: float32 [1536, 1536], P(('kv', 'qh'), 'seq')
- mlp_gain_grad: float32 [1536], replicated
- gate_weight_grad: float32 [1536, 8960], P('seq', ('kv', 'qh'))
- up_weight_grad: float32 [1536, 8960], P('seq', ('kv', 'qh'))
- down_weight_grad: float32 [8960, 1536], P(('kv', 'qh'), 'seq')
Inputs may be any that keep to these rules, and one draw needn't show every extreme that they name: `segment_ids`: along each row the ids start at 0 and never fall. `position_ids`: count from 0 at the first token of each run of equal segment ids and rise by one within it.
All inputs are finite; a program needn't handle non-finite values.
Results may differ from a plain program's by a relative error of at most 0.035.
Values may be sent and summed in bfloat16 or wider, within the bound.
A program may use at most 320 MiB of HBM per device.

v0:
```python
import jax
import jax.numpy as jnp
from jax import lax
from jax.sharding import PartitionSpec as P

epsilon = 1e-06
rope_base = 1000000.0


def angles(positions, head_width):
    indices = jnp.arange(head_width // 2, dtype=jnp.float32)
    inverse = 1.0 / jnp.power(rope_base, indices * 2.0 / head_width)
    phase_angle = positions.astype(jnp.float32)[..., None] * inverse
    return (jnp.cos(phase_angle), jnp.sin(phase_angle))


def rotate(vectors, cosine, sine):
    half_width = vectors.shape[-1] // 2
    first_half = vectors[..., :half_width]
    second = vectors[..., half_width:]
    return jnp.concatenate(
        [first_half * cosine - second * sine, second * cosine + first_half * sine], axis=-1
    )


def normalize(vectors, gain_vec):
    inv_rms = lax.rsqrt(jnp.mean(vectors * vectors, axis=-1, keepdims=True) + epsilon)
    return (vectors * inv_rms * gain_vec, inv_rms)


def normalize_back(vectors, inv_rms, gain_vec, grad_in):
    weighted = grad_in * gain_vec
    inner_mean = jnp.mean(vectors * weighted, axis=-1, keepdims=True)
    back = inv_rms * weighted - vectors * inv_rms * inv_rms * inv_rms * inner_mean
    return (back, jnp.sum(grad_in * vectors * inv_rms, axis=(0, 1)))


def grouped(array):
    return array.reshape((array.shape[0] // 2, 2) + array.shape[1:])


def ungroup(array):
    return array.reshape((array.shape[0] * 2,) + array.shape[2:])


def visible(query_order, query_segs, key_order, key_segs):
    return (key_order[None, None, :] <= query_order[None, :, None]) & (
        query_segs[:, :, None] == key_segs[:, None, :]
    )


def attend_forward(
    queries, key_row_block, value_row_block, query_order, query_segs, key_order, key_segs
):
    scaling = queries.shape[-1] ** (-0.5)
    scores = (
        jnp.einsum("rqhd,rkd->rhqk", queries, key_row_block, preferred_element_type=jnp.float32)
        * scaling
    )
    allowed = visible(query_order, query_segs, key_order, key_segs)
    scores = jnp.where(allowed[:, None], scores, -1e30)
    row_max = jnp.max(scores, axis=-1, keepdims=True)
    exponent = jnp.exp(scores - row_max)
    row_total = jnp.sum(exponent, axis=-1, keepdims=True)
    probs_low = (exponent / row_total).astype(jnp.bfloat16)
    context = jnp.einsum(
        "rhqk,rkd->rqhd", probs_low, value_row_block, preferred_element_type=jnp.float32
    )
    return (context, (row_max + jnp.log(row_total))[..., 0])


def score_grads(
    queries,
    grad_out,
    logsum,
    inner_sum,
    query_order,
    query_segs,
    key_row_block,
    value_row_block,
    key_order,
    key_segs,
):
    scaling = queries.shape[-1] ** (-0.5)
    scores = (
        jnp.einsum("rqhd,rkd->rhqk", queries, key_row_block, preferred_element_type=jnp.float32)
        * scaling
    )
    allowed = visible(query_order, query_segs, key_order, key_segs)
    probs = jnp.where(allowed[:, None], jnp.exp(scores - logsum[..., None]), 0.0)
    grad_probs = jnp.einsum(
        "rqhd,rkd->rhqk", grad_out, value_row_block, preferred_element_type=jnp.float32
    )
    grad_scores = (probs * (grad_probs - inner_sum[..., None])).astype(jnp.bfloat16)
    return (probs.astype(jnp.bfloat16), grad_scores, scaling)


def both_sides(
    queries,
    grad_out,
    logsum,
    inner_sum,
    query_order,
    query_segs,
    key_row_block,
    value_row_block,
    key_order,
    key_segs,
):
    probs_low, grad_scores, scaling = score_grads(
        queries,
        grad_out,
        logsum,
        inner_sum,
        query_order,
        query_segs,
        key_row_block,
        value_row_block,
        key_order,
        key_segs,
    )
    grad_queries = (
        jnp.einsum("rhqk,rkd->rqhd", grad_scores, key_row_block, preferred_element_type=jnp.float32)
        * scaling
    )
    grad_keys = (
        jnp.einsum("rhqk,rqhd->rkd", grad_scores, queries, preferred_element_type=jnp.float32)
        * scaling
    )
    grad_values = jnp.einsum(
        "rhqk,rqhd->rkd", probs_low, grad_out, preferred_element_type=jnp.float32
    )
    return (grad_queries, grad_keys, grad_values)


def local(
    tokens,
    attn_gain,
    query_weight,
    query_bias,
    key_matrix,
    key_offset_bias,
    value_matrix,
    value_offset_bias,
    out_weight,
    mlp_gain,
    gate_weight,
    up_weight,
    down_weight,
    segment_ids,
    position_ids,
    cotangent,
):
    tok_span = tokens.shape[1]
    head_dim = key_matrix.shape[1]
    local_width = query_weight.shape[1]
    local_heads = local_width // head_dim
    seq_start = lax.axis_index("seq") * tok_span
    query_order = seq_start + jnp.arange(tok_span, dtype=jnp.int32)
    key_order = jnp.arange(segment_ids.shape[1], dtype=jnp.int32)
    query_segs = lax.dynamic_slice_in_dim(segment_ids, seq_start, tok_span, 1)
    gain_one = attn_gain.astype(jnp.float32)
    gain_two = mlp_gain.astype(jnp.float32)
    inputs = tokens.astype(jnp.float32)
    normed_one, factor_one = normalize(inputs, gain_one)
    gathered_one = lax.all_gather(normed_one.astype(jnp.bfloat16), ("kv", "qh"), axis=0, tiled=True)
    row_count = gathered_one.shape[0]
    cosine, sine = angles(position_ids, head_dim)
    query_lin = jnp.dot(
        gathered_one, query_weight, preferred_element_type=jnp.float32
    ) + query_bias.astype(jnp.float32)
    query_rot = rotate(
        query_lin.reshape(row_count, tok_span, local_heads, head_dim),
        cosine[:, :, None],
        sine[:, :, None],
    ).astype(jnp.bfloat16)
    key_lin = jnp.dot(
        gathered_one, key_matrix, preferred_element_type=jnp.float32
    ) + key_offset_bias.astype(jnp.float32)
    key_rot = rotate(key_lin, cosine, sine).astype(jnp.bfloat16)
    value_low = (
        jnp.dot(gathered_one, value_matrix, preferred_element_type=jnp.float32)
        + value_offset_bias.astype(jnp.float32)
    ).astype(jnp.bfloat16)
    keys_all, values_all = (
        lax.all_gather(key_rot, "seq", axis=1, tiled=True),
        lax.all_gather(value_low, "seq", axis=1, tiled=True),
    )

    def forward_group(pieces):
        return attend_forward(
            pieces[0], pieces[1], pieces[2], query_order, pieces[3], key_order, pieces[4]
        )

    context, logsum = lax.map(
        forward_group,
        (
            grouped(query_rot),
            grouped(keys_all),
            grouped(values_all),
            grouped(query_segs),
            grouped(segment_ids),
        ),
    )
    context = ungroup(context)
    logsum = ungroup(logsum)
    context_low = context.reshape(row_count, tok_span, local_width).astype(jnp.bfloat16)
    branch = jnp.dot(context_low, out_weight, preferred_element_type=jnp.float32)
    hidden = inputs + lax.psum_scatter(
        branch.astype(jnp.bfloat16), ("kv", "qh"), scatter_dimension=0, tiled=True
    ).astype(jnp.float32)
    normed_two, factor_two = normalize(hidden, gain_two)
    gathered_two = lax.all_gather(normed_two.astype(jnp.bfloat16), ("kv", "qh"), axis=0, tiled=True)
    gate_val = jnp.dot(gathered_two, gate_weight, preferred_element_type=jnp.float32)
    up_val = jnp.dot(gathered_two, up_weight, preferred_element_type=jnp.float32)
    sigmoid_gate = jax.nn.sigmoid(gate_val)
    silu_gate = gate_val * sigmoid_gate
    activation = (silu_gate * up_val).astype(jnp.bfloat16)
    mlp_part = jnp.dot(activation, down_weight, preferred_element_type=jnp.float32)
    output = (
        hidden
        + lax.psum_scatter(
            mlp_part.astype(jnp.bfloat16), ("kv", "qh"), scatter_dimension=0, tiled=True
        ).astype(jnp.float32)
    ).astype(jnp.bfloat16)
    grad_rows = lax.all_gather(cotangent, ("kv", "qh"), axis=0, tiled=True)
    down_grad = jnp.einsum("rtf,rtd->fd", activation, grad_rows, preferred_element_type=jnp.float32)
    grad_act = jnp.einsum("rtd,fd->rtf", grad_rows, down_weight, preferred_element_type=jnp.float32)
    grad_gate = (grad_act * up_val * sigmoid_gate * (1.0 + gate_val * (1.0 - sigmoid_gate))).astype(
        jnp.bfloat16
    )
    grad_up = (grad_act * silu_gate).astype(jnp.bfloat16)
    gate_grad = jnp.einsum(
        "rtd,rtf->df", gathered_two, grad_gate, preferred_element_type=jnp.float32
    )
    up_grad = jnp.einsum("rtd,rtf->df", gathered_two, grad_up, preferred_element_type=jnp.float32)
    normed_grad_part = jnp.einsum(
        "rtf,df->rtd", grad_gate, gate_weight, preferred_element_type=jnp.float32
    ) + jnp.einsum("rtf,df->rtd", grad_up, up_weight, preferred_element_type=jnp.float32)
    normed_grad_two = lax.psum_scatter(
        normed_grad_part.astype(jnp.bfloat16), ("kv", "qh"), scatter_dimension=0, tiled=True
    ).astype(jnp.float32)
    back_two, gain_two_part = normalize_back(hidden, factor_two, gain_two, normed_grad_two)
    grad_hidden = cotangent.astype(jnp.float32) + back_two
    grad_branch = lax.all_gather(grad_hidden.astype(jnp.bfloat16), ("kv", "qh"), axis=0, tiled=True)
    out_grad = jnp.einsum(
        "rtc,rtd->cd", context_low, grad_branch, preferred_element_type=jnp.float32
    )
    grad_context = jnp.einsum(
        "rtd,cd->rtc", grad_branch, out_weight, preferred_element_type=jnp.float32
    )
    grad_context = grad_context.astype(jnp.bfloat16).reshape(
        row_count, tok_span, local_heads, head_dim
    )
    inner_sum = jnp.einsum("rthd,rthd->rht", grad_context.astype(jnp.float32), context)

    def returned_group(pieces):
        return both_sides(
            pieces[0],
            pieces[1],
            pieces[2],
            pieces[3],
            query_order,
            pieces[4],
            pieces[5],
            pieces[6],
            key_order,
            pieces[7],
        )

    grad_query, grad_keys_all, grad_values_all = lax.map(
        returned_group,
        (
            grouped(query_rot),
            grouped(grad_context),
            grouped(logsum),
            grouped(inner_sum),
            grouped(query_segs),
            grouped(keys_all),
            grouped(values_all),
            grouped(segment_ids),
        ),
    )
    grad_query = ungroup(grad_query)
    grad_keys, grad_values = (
        lax.psum_scatter(
            ungroup(grad_keys_all).astype(jnp.bfloat16), "seq", scatter_dimension=1, tiled=True
        ).astype(jnp.float32),
        lax.psum_scatter(
            ungroup(grad_values_all).astype(jnp.bfloat16), "seq", scatter_dimension=1, tiled=True
        ).astype(jnp.float32),
    )
    grad_key_lin = rotate(grad_keys, cosine, -sine).astype(jnp.bfloat16)
    grad_value_lin = grad_values.astype(jnp.bfloat16)
    grad_query_lin = rotate(grad_query, cosine[:, :, None], -sine[:, :, None]).astype(jnp.bfloat16)
    grad_query_lin = grad_query_lin.reshape(row_count, tok_span, local_width)
    query_grad = jnp.einsum(
        "rtd,rtc->dc", gathered_one, grad_query_lin, preferred_element_type=jnp.float32
    )
    key_part = jnp.einsum(
        "rtd,rtc->dc", gathered_one, grad_key_lin, preferred_element_type=jnp.float32
    )
    value_part = jnp.einsum(
        "rtd,rtc->dc", gathered_one, grad_value_lin, preferred_element_type=jnp.float32
    )
    normed_grad_part = (
        jnp.einsum("rtc,dc->rtd", grad_query_lin, query_weight, preferred_element_type=jnp.float32)
        + jnp.einsum("rtc,dc->rtd", grad_key_lin, key_matrix, preferred_element_type=jnp.float32)
        + jnp.einsum(
            "rtc,dc->rtd", grad_value_lin, value_matrix, preferred_element_type=jnp.float32
        )
    )
    normed_grad_one = lax.psum_scatter(
        normed_grad_part.astype(jnp.bfloat16), ("kv", "qh"), scatter_dimension=0, tiled=True
    ).astype(jnp.float32)
    back_one, gain_one_part = normalize_back(inputs, factor_one, gain_one, normed_grad_one)
    tokens_grad = grad_hidden + back_one
    head_slot = lax.axis_index(("kv", "qh")) * local_width
    group_slot = lax.axis_index("kv") * head_dim
    group_width = head_dim * lax.axis_size("kv")
    query_bias_full = lax.dynamic_update_slice_in_dim(
        jnp.zeros((local_width * lax.axis_size(("kv", "qh")),), jnp.float32),
        jnp.sum(grad_query_lin.astype(jnp.float32), axis=(0, 1)),
        head_slot,
        0,
    )
    key_bias_full = lax.dynamic_update_slice_in_dim(
        jnp.zeros((group_width,), jnp.float32),
        jnp.sum(grad_key_lin.astype(jnp.float32), axis=(0, 1)),
        group_slot,
        0,
    )
    value_bias_full = lax.dynamic_update_slice_in_dim(
        jnp.zeros((group_width,), jnp.float32),
        jnp.sum(grad_value_lin.astype(jnp.float32), axis=(0, 1)),
        group_slot,
        0,
    )
    key_weight_full = lax.dynamic_update_slice_in_dim(
        jnp.zeros((key_matrix.shape[0], group_width), jnp.float32), key_part, group_slot, 1
    )
    value_weight_full = lax.dynamic_update_slice_in_dim(
        jnp.zeros((key_matrix.shape[0], group_width), jnp.float32), value_part, group_slot, 1
    )
    small_totals = lax.psum(
        (
            gain_one_part,
            gain_two_part,
            query_bias_full,
            key_bias_full,
            value_bias_full,
            key_weight_full,
            value_weight_full,
        ),
        ("kv", "qh", "seq"),
    )
    weight_totals = (
        lax.psum_scatter(
            query_grad.astype(jnp.bfloat16), "seq", scatter_dimension=0, tiled=True
        ).astype(jnp.float32),
        lax.psum_scatter(
            out_grad.astype(jnp.bfloat16), "seq", scatter_dimension=1, tiled=True
        ).astype(jnp.float32),
        lax.psum_scatter(
            gate_grad.astype(jnp.bfloat16), "seq", scatter_dimension=0, tiled=True
        ).astype(jnp.float32),
        lax.psum_scatter(
            up_grad.astype(jnp.bfloat16), "seq", scatter_dimension=0, tiled=True
        ).astype(jnp.float32),
        lax.psum_scatter(
            down_grad.astype(jnp.bfloat16), "seq", scatter_dimension=1, tiled=True
        ).astype(jnp.float32),
    )
    return (
        output,
        tokens_grad,
        small_totals[0],
        weight_totals[0],
        small_totals[2],
        small_totals[5],
        small_totals[3],
        small_totals[6],
        small_totals[4],
        weight_totals[1],
        small_totals[1],
        weight_totals[2],
        weight_totals[3],
        weight_totals[4],
    )


def solution(mesh):
    return jax.shard_map(
        local,
        mesh=mesh,
        in_specs=(
            P(("kv", "qh"), "seq", None),
            P(),
            P(None, ("kv", "qh")),
            P(("kv", "qh")),
            P(None, "kv"),
            P("kv"),
            P(None, "kv"),
            P("kv"),
            P(("kv", "qh"), None),
            P(),
            P(None, ("kv", "qh")),
            P(None, ("kv", "qh")),
            P(("kv", "qh"), None),
            P(),
            P(None, "seq"),
            P(("kv", "qh"), "seq", None),
        ),
        out_specs=(
            P(("kv", "qh"), "seq", None),
            P(("kv", "qh"), "seq", None),
            P(),
            P("seq", ("kv", "qh")),
            P(),
            P(),
            P(),
            P(),
            P(),
            P(("kv", "qh"), "seq"),
            P(),
            P("seq", ("kv", "qh")),
            P("seq", ("kv", "qh")),
            P(("kv", "qh"), "seq"),
        ),
        check_vma=False,
    )
```

profile of v0, /device:TPU:0, one launch (start us, length us, event | category | flops | bytes accessed | tf_op | source)
XLA Modules:
  0.0 1125.8 jit_solution(11208515343573073030)
XLA Ops:
  9.5 2.3 fusion.97
  11.9 46.7 %all-gather.7.cloned.1.call-done = bf16[8,128,1536]{2,1,0:T(8,128)(2,1)} async-done(((bf16[2,128,1536]{2,1,0:T(8,128)(2,1)}), bf16[8,128,1536]{2,1,0:T(8,128)(2,1)}) %all-gather.7.cloned.1.call-update) | async-done | bytes 3145744 | tf_op jit(solution)/shard_map/all_gather | solution.py:166
  58.6 3.1 convolution_add_fusion.1
  64.4 3.6 fusion.112
  68.7 4.8 convolution_add_fusion
  79.8 15.5 %all-gather.11.cloned.1.call-done = bf16[8,1024,128]{1,2,0:T(8,128)(2,1)} async-done(((bf16[8,128,128]{1,2,0:T(8,128)(2,1)}), bf16[8,1024,128]{1,2,0:T(8,128)(2,1)}) %all-gather.11.cloned.1.call-update) | async-done | bytes 2097168 | tf_op jit(solution)/shard_map/all_gather | solution.py:186
  95.3 3.9 copy.92
  99.2 26.5 %all-gather.9.cloned.1.call-done = bf16[8,1024,128]{2,1,0:T(8,128)(2,1)} async-done(((bf16[8,128,128]{2,1,0:T(8,128)(2,1)}), bf16[8,1024,128]{2,1,0:T(8,128)(2,1)}) %all-gather.9.cloned.1.call-update) | async-done | bytes 2097168 | tf_op jit(solution)/shard_map/all_gather | solution.py:187
  127.0 28.3 %while.28 = (s32[]{:T(128)}, f32[4,2,128,3,128]{2,4,3,1,0:T(8,128)}, f32[4,2,3,128]{3,2,1,0:T(4,128)}, bf16[4,2,1024,128]{3,2,1,0:T(8,128)(2,1)}, s32[4,2,128]{2...) while((s32[]{:T(128)}, ...), condition=%wide.region_4.5_spmd.clone, body=%wide.region_1.4_spmd.clone.sunk | while | flops 412745088 | bytes 12443249 | solution.py:195
  131.3 2.8 fusion.194
  138.3 2.8 fusion.194
  145.4 2.8 fusion.194
  152.5 2.8 fusion.194
  157.7 3.5 convolution_convert_fusion
  161.9 42.9 %reduce-scatter.14.cloned.1.call-done = bf16[2,128,1536]{2,1,0:T(8,128)(2,1)} async-done(((bf16[8,128,1536]{2,1,0:T(8,128)(2,1)}), bf16[2,128,1536]{2,1,0:T(8,128)(2,1)}) %reduce-scatter.14.cloned.1.call-update) | async-done | bytes 786448 | tf_op jit(solution)/shard_map/reduce_scatter | solution.py:209
  206.3 2.3 multiply_convert_fusion.3
  209.2 41.3 %all-gather.15.cloned.1.call-done = bf16[8,128,1536]{2,1,0:T(8,128)(2,1)} async-done(((bf16[2,128,1536]{2,1,0:T(8,128)(2,1)}), bf16[8,128,1536]{2,1,0:T(8,128)(2,1)}) %all-gather.15.cloned.1.call-update) | async-done | bytes 3145744 | tf_op jit(solution)/shard_map/all_gather | solution.py:226
  250.5 12.1 %fusion.71 = f32[8,128,2240]{1,2,0:T(8,128)} fusion(bf16[8,128,1536]{2,1,0:T(8,128)(2,1)} %all-gather.15.cloned.1.call-done, bf16[2240,1536]{1,0:T(8,128)(2,1)} %param.32), kind=kOutput, calls=%fused_computation.89 | convolution fusion | flops 7046430720 | bytes 19202048 | tf_op jit(solution)/shard_map/rtd,fd->rtf/dot_general | solution.py:228
  262.6 34.1 %all-gather.13.cloned.1.call-done = bf16[8,128,1536]{2,1,0:T(8,128)(2,1)} async-done(((bf16[2,128,1536]{2,1,0:T(8,128)(2,1)}), bf16[8,128,1536]{2,1,0:T(8,128)(2,1)}) %all-gather.13.cloned.1.call-update) | async-done | bytes 3145744 | tf_op jit(solution)/shard_map/all_gather | solution.py:213
  296.8 12.7 %fusion.77 = f32[8,128,2240]{1,2,0:T(8,128)} fusion(bf16[8,128,1536]{2,1,0:T(8,128)(2,1)} %all-gather.13.cloned.1.call-done, bf16[1536,2240]{0,1:T(8,128)(2,1)} %param.31), kind=kOutput, calls=%fused_computation.95 | convolution fusion | flops 7046430720 | bytes 19202048 | tf_op jit(solution)/shard_map/dot_general | solution.py:215
  309.4 18.7 %multiply_convert_fusion.1 = (bf16[8,128,2240]{1,2,0:T(8,128)(2,1)}, bf16[8,128,2240]{1,2,0:T(8,128)(2,1)}, bf16[8,128,2240]{1,2,0:T(8,128)(2,1)}) fusion(f32[8,128,2240]{1,2,0:T(8,128)} %fusion.71, f32[8,128,2240]{1,2,0:T(8,128)} %fusion.77, bf16[8,128,1536]{2,1,0:T(8,128)(2,1)S(1)} %copy-done.37, bf16[1536,2240]{0,1:T(8,128)(2,1)} %param.30), kind=kOutput, calls=%fused_computation.85 | convolution fusion | flops 7080837120 | bytes 42139648 | tf_op jit(solution)/shard_map/dot_general | solution.py:214
  328.2 11.6 %fusion.75 = f32[8,128,1536]{2,1,0:T(8,128)S(1)} fusion(bf16[8,128,2240]{1,2,0:T(8,128)(2,1)} %get-tuple-element.326, bf16[1536,2240]{0,1:T(8,128)(2,1)} %param.31), kind=kOutput, calls=%fused_computation.93 | convolution fusion | flops 7046430720 | bytes 17760256 | tf_op jit(solution)/shard_map/rtf,df->rtd/dot_general | solution.py:239
  339.8 11.4 %add_convert_fusion.1 = bf16[8,128,1536]{2,1,0:T(8,128)(2,1)} fusion(f32[8,128,1536]{2,1,0:T(8,128)S(1)} %fusion.75, bf16[8,128,2240]{1,2,0:T(8,128)(2,1)S(1)} %copy-done.40, bf16[1536,2240]{0,1:T(8,128)(2,1)} %param.30), kind=kOutput, calls=%fused_computation.102 | convolution fusion | flops 7049576448 | bytes 20905984 | tf_op jit(solution)/shard_map/rtf,df->rtd/dot_general | solution.py:237
  351.3 44.1 %reduce-scatter.18.cloned.1.call-done = bf16[2,128,1536]{2,1,0:T(8,128)(2,1)} async-done(((bf16[8,128,1536]{2,1,0:T(8,128)(2,1)}), bf16[2,128,1536]{2,1,0:T(8,128)(2,1)}) %reduce-scatter.18.cloned.1.call-update) | async-done | bytes 786448 | tf_op jit(solution)/shard_map/reduce_scatter | solution.py:240
  395.4 2.3 fusion.106
  398.2 3.0 fusion.127
  401.2 44.0 %all-gather.17.cloned.1.call-done = bf16[8,128,1536]{2,1,0:T(8,128)(2,1)} async-done(((bf16[2,128,1536]{2,1,0:T(8,128)(2,1)}), bf16[8,128,1536]{2,1,0:T(8,128)(2,1)}) %all-gather.17.cloned.1.call-update) | async-done | bytes 3145744 | tf_op jit(solution)/shard_map/all_gather | solution.py:245
  445.3 4.6 convolution_convert_fusion.1
  451.3 2.2 fusion.111
  454.9 44.1 %while.29 = (s32[]{:T(128)}, f32[4,2,128,3,128]{2,4,3,1,0:T(8,128)}, bf16[4,2,1024,128]{3,2,1,0:T(8,128)(2,1)}, bf16[4,2,1024,128]{3,2,1,0:T(8,128)(2,1)}, bf16[...) while((s32[]{:T(128)}, ...), condition=%wide.region_11.12_spmd.clone, body=%wide.region_10.11_spmd.clone.sunk | while | flops 1015513216 | bytes 36889804 | solution.py:271
  458.7 2.3 fusion.207
  461.7 2.7 fusion.208
  469.6 2.3 fusion.207
  472.7 2.7 fusion.208
  480.6 2.3 fusion.207
  483.7 2.7 fusion.208
  491.6 2.3 fusion.207
  494.6 2.7 fusion.208
  498.9 2.9 copy.145
  505.0 4.7 fusion.89
  509.8 12.4 %bitcast_convert_fusion.2 = bf16[1536,2240]{1,0:T(8,128)(2,1)} fusion(bf16[8,128,1536]{2,1,0:T(8,128)(2,1)} %all-gather.13.cloned.1.call-done, bf16[8,128,2240]{1,2,0:T(8,128)(2,1)} %get-tuple-element.325), kind=kOutput, calls=%fused_computation.83 | convolution fusion | flops 7049871360 | bytes 14614528 | tf_op jit(solution)/shard_map/rtd,rtf->df/dot_general | solution.py:233
  522.3 12.7 %bitcast_convert_fusion.1 = bf16[1536,2240]{1,0:T(8,128)(2,1)} fusion(bf16[8,128,1536]{2,1,0:T(8,128)(2,1)} %all-gather.13.cloned.1.call-done, bf16[8,128,2240]{1,2,0:T(8,128)(2,1)} %get-tuple-element.326), kind=kOutput, calls=%fused_computation.82 | convolution fusion | flops 7049871360 | bytes 14614528 | tf_op jit(solution)/shard_map/rtd,rtf->df/dot_general | solution.py:236
  535.1 12.4 %bitcast_convert_fusion = bf16[2240,1536]{0,1:T(8,128)(2,1)} fusion(bf16[8,128,2240]{1,2,0:T(8,128)(2,1)} %get-tuple-element.327, bf16[8,128,1536]{2,1,0:T(8,128)(2,1)} %all-gather.15.cloned.1.call-done), kind=kOutput, calls=%fused_computation.81 | convolution fusion | flops 7049871360 | bytes 14614528 | tf_op jit(solution)/shard_map/rtf,rtd->fd/dot_general | solution.py:227
  552.6 2.9 fusion.88
  556.0 3.6 fusion.118
  559.6 4.5 fusion.115
  564.2 12.3 %reduce-scatter.20.cloned.1.call-done = bf16[8,128,128]{2,1,0:T(8,128)(2,1)} async-done(((bf16[8,1024,128]{2,1,0:T(8,128)(2,1)}), bf16[8,128,128]{2,1,0:T(8,128)(2,1)}) %reduce-scatter.20.cloned.1.call-update) | async-done | bytes 262160 | tf_op jit(solution)/shard_map/reduce_scatter | solution.py:289
  576.4 7.3 add_convert_fusion
  583.8 12.4 %fusion.85 = bf16[8,128,1536]{2,1,0:T(8,128)(2,1)} fusion(bf16[8,128,2240]{1,2,0:T(8,128)(2,1)} %get-tuple-element.327, bf16[2240,1536]{1,0:T(8,128)(2,1)} %param.32), kind=kOutput, calls=%fused_computation.103 | convolution fusion | flops 7048003584 | bytes 14614528 | tf_op jit(solution)/shard_map/dot_general | solution.py:219
  597.5 4.0 fusion.91
  604.7 6.0 reduce-scatter.26.cloned.1.call-done
  612.4 76.1 %reduce-scatter.28.cloned.1.call-done = bf16[192,2240]{1,0:T(8,128)(2,1)} async-done(((bf16[1536,2240]{1,0:T(8,128)(2,1)}), bf16[192,2240]{1,0:T(8,128)(2,1)}) %reduce-scatter.28.cloned.1.call-update) | async-done | bytes 860176 | tf_op jit(solution)/shard_map/reduce_scatter | solution.py:364
  688.4 2.5 convert_element_type.202
  690.9 75.4 %reduce-scatter.30.cloned.1.call-done = bf16[192,2240]{1,0:T(8,128)(2,1)} async-done(((bf16[1536,2240]{1,0:T(8,128)(2,1)}), bf16[192,2240]{1,0:T(8,128)(2,1)}) %reduce-scatter.30.cloned.1.call-update) | async-done | bytes 860176 | tf_op jit(solution)/shard_map/reduce_scatter | solution.py:367
  766.4 2.5 convert_element_type.204
  768.9 75.3 %reduce-scatter.32.cloned.1.call-done = bf16[2240,192]{0,1:T(8,128)(2,1)} async-done(((bf16[2240,1536]{0,1:T(8,128)(2,1)}), bf16[2240,192]{0,1:T(8,128)(2,1)}) %reduce-scatter.32.cloned.1.call-update) | async-done | bytes 860176 | tf_op jit(solution)/shard_map/reduce_scatter | solution.py:370
  844.2 2.5 convert_element_type.206
  850.2 27.7 %reduce-scatter.24.cloned.1.call-done = bf16[192,384]{1,0:T(8,128)(2,1)} async-done(((bf16[1536,384]{1,0:T(8,128)(2,1)}), bf16[192,384]{1,0:T(8,128)(2,1)}) %reduce-scatter.24.cloned.1.call-update) | async-done | bytes 147472 | tf_op jit(solution)/shard_map/reduce_scatter | solution.py:358
  879.5 43.6 %reduce-scatter.22.cloned.1.call-done = bf16[2,128,1536]{2,1,0:T(8,128)(2,1)} async-done(((bf16[8,128,1536]{2,1,0:T(8,128)(2,1)}), bf16[2,128,1536]{2,1,0:T(8,128)(2,1)}) %reduce-scatter.22.cloned.1.call-update) | async-done | bytes 786448 | tf_op jit(solution)/shard_map/reduce_scatter | solution.py:313
  924.7 40.6 %all-reduce = (f32[1536]{0:T(1024)}, f32[1536]{0:T(1024)}, f32[256]{0:T(256)}, f32[256]{0:T(256)}, f32[1536]{0:T(1024)}) all-reduce(f32[1536]{0:T(1024)S(1)} %get-tuple-element.266, f32[1536]{0:T(1024)S(1)} %bitcast_dynamic-update-slice_fusion.1, ...), channel_id=1, replica_groups=mesh['kv'=2,'qh'=2,'seq'=8] {'kv','qh','seq'}, use_global_device_ids=true, to_apply=%region_17.18 | all-reduce | flops 5120 | bytes 40960 | tf_op jit(solution)/shard_map/psum | solution.py:345
  965.3 5.3 reduce-scatter.16.cloned.1.call-done
  970.7 4.2 fusion.101
  974.9 139.9 %all-reduce.4.cloned.1.call-done = (f32[1536,256]{1,0:T(8,128)}, f32[1536,256]{1,0:T(8,128)}) async-done(((f32[1536,256]{1,0:T(8,128)}, f32[1536,256]{1,0:T(8,128)}), (f32[1536,256]{1,0:T(8,128)}, f32[1536,256]{1,0:T(8,128)})) %all-reduce.4.cloned.1.call-update) | async-done | bytes 3145744 | tf_op jit(solution)/shard_map/psum | solution.py:345
  1114.8 2.8 copy.188
  (250 shorter events, 85.5 us)
Async XLA Ops:
  7.2 150.6 %copy-start = (bf16[384,1536]{1,0:T(8,128)(2,1)S(1)}, bf16[384,1536]{1,0:T(8,128)(2,1)}, u32[]{:S(2)}) copy-start(bf16[384,1536]{1,0:T(8,128)(2,1)} %param.28) | copy-start | bytes 3538948
  7.2 4.6 copy-start.38
  7.2 4.6 copy-start.33
  7.2 51.4 %copy-start.17 = (bf16[1536,128]{1,0:T(8,128)(2,1)S(1)}, bf16[1536,128]{1,0:T(8,128)(2,1)}, u32[]{:S(2)}) copy-start(bf16[1536,128]{1,0:T(8,128)(2,1)} %param.24) | copy-start | bytes 1179652
  7.2 51.3 %all-gather.7.cloned.1.call-start = ((), (), s32[]{:S(2)}) async-start(), calls=%async_computation.11 | async-start | bytes 3932160 | tf_op jit(solution)/shard_map/all_gather | solution.py:166
  8.1 50.5 %copy-start.24 = (f32[1536]{0:T(1024)}, f32[1536]{0:T(1024)S(1)}, u32[]{:S(2)}) copy-start(f32[1536]{0:T(1024)S(1)} %convert_element_type.161) | copy-start | bytes 18436
  9.5 49.1 %copy-start.30 = (f32[2,128]{1,0:T(2,128)}, f32[2,128]{1,0:T(2,128)S(1)}, u32[]{:S(2)}) copy-start(f32[2,128]{1,0:T(2,128)S(1)} %add_rsqrt_fusion.1) | copy-start | bytes 3076
  11.7 52.6 %copy-start.39 = (bf16[128]{0:T(256)(128)(2,1)S(1)}, bf16[128]{0:T(256)(128)(2,1)}, u32[]{:S(2)}) copy-start(bf16[128]{0:T(256)(128)(2,1)} %param.27) | copy-start | bytes 772
  11.8 52.6 %copy-start.22 = (bf16[1536,128]{1,0:T(8,128)(2,1)S(1)}, bf16[1536,128]{1,0:T(8,128)(2,1)}, u32[]{:S(2)}) copy-start(bf16[1536,128]{1,0:T(8,128)(2,1)} %param.26) | copy-start | bytes 1179652
  11.8 83.5 %all-gather.11.cloned.1.call-start = ((), (), s32[]{:S(2)}) async-start(), calls=%async_computation.13 | async-start | bytes 2359296 | tf_op jit(solution)/shard_map/all_gather | solution.py:186
  11.9 56.1 %copy-start.27 = (f32[8,128]{1,0:T(8,128)}, f32[8,128]{1,0:T(8,128)S(1)}, u32[]{:S(2)}) copy-start(f32[8,128]{1,0:T(8,128)S(1)} %convert_element_type.166) | copy-start | bytes 12292
  11.9 56.1 %copy-start.34 = (f32[64]{0:T(128)}, f32[64]{0:T(128)S(1)}, u32[]{:S(2)}) copy-start(f32[64]{0:T(128)S(1)} %negate_power_fusion) | copy-start | bytes 772
  61.6 6.4 copy-start.36
  61.7 7.1 copy-start.19
  63.5 12.0 %copy-start.11 = (f32[8,128,64]{1,2,0:T(8,128)}, f32[8,128,64]{1,2,0:T(8,128)S(1)}, u32[]{:S(2)}) copy-start(f32[8,128,64]{1,2,0:T(8,128)S(1)} %get-tuple-element.339) | copy-start | bytes 786436
  63.5 4.6 copy-start.26
  64.3 61.4 %all-gather.9.cloned.1.call-start = ((), (), s32[]{:S(2)}) async-start(), calls=%async_computation.12 | async-start | bytes 2359296 | tf_op jit(solution)/shard_map/all_gather | solution.py:187
  68.0 136.8 %reduce-scatter.14.cloned.1.call-start = ((), (), s32[]{:S(2)}) async-start(), calls=%async_computation.14 | async-start | bytes 3932160 | tf_op jit(solution)/shard_map/reduce_scatter | solution.py:209
  73.6 1.9 copy-start.21
  156.8 0.9 copy-start.8
  161.2 0.7 copy-start.32
  161.2 43.6 %copy-start.2 = (bf16[2,128,1536]{2,1,0:T(8,128)(2,1)S(1)}, bf16[2,128,1536]{2,1,0:T(8,128)(2,1)}, u32[]{:S(2)}) copy-start(bf16[2,128,1536]{2,1,0:T(8,128)(2,1)} %param.20) | copy-start | bytes 2359300
  161.2 89.3 %all-gather.15.cloned.1.call-start = ((), (), s32[]{:S(2)}) async-start(), calls=%async_computation.17 | async-start | bytes 3932160 | tf_op jit(solution)/shard_map/all_gather | solution.py:226
  161.8 135.0 %all-gather.13.cloned.1.call-start = ((), (), s32[]{:S(2)}) async-start(), calls=%async_computation.15 | async-start | bytes 3932160 | tf_op jit(solution)/shard_map/all_gather | solution.py:213
  206.3 191.3 %copy-start.29 = (f32[2,128]{1,0:T(2,128)}, f32[2,128]{1,0:T(2,128)S(1)}, u32[]{:S(2)}) copy-start(f32[2,128]{1,0:T(2,128)S(1)} %add_rsqrt_fusion) | copy-start | bytes 3076
  208.6 186.7 %reduce-scatter.18.cloned.1.call-start = ((), (), s32[]{:S(2)}) async-start(), calls=%async_computation.18 | async-start | bytes 3932160 | tf_op jit(solution)/shard_map/reduce_scatter | solution.py:240
  296.8 12.7 %copy-start.37 = (bf16[8,128,1536]{2,1,0:T(8,128)(2,1)S(1)}, bf16[8,128,1536]{2,1,0:T(8,128)(2,1)}, u32[]{:S(2)}) copy-start(bf16[8,128,1536]{2,1,0:T(8,128)(2,1)} %all-gather.13.cloned.1.call-done) | copy-start | bytes 9437188
  328.2 11.7 %copy-start.40 = (bf16[8,128,2240]{1,2,0:T(8,128)(2,1)S(1)}, bf16[8,128,2240]{1,2,0:T(8,128)(2,1)}, u32[]{:S(2)}) copy-start(bf16[8,128,2240]{1,2,0:T(8,128)(2,1)} %get-tuple-element.325) | copy-start | bytes 13762564
  351.2 44.1 %copy-start.5 = (bf16[2,128,1536]{2,1,0:T(8,128)(2,1)S(1)}, bf16[2,128,1536]{2,1,0:T(8,128)(2,1)}, u32[]{:S(2)}) copy-start(bf16[2,128,1536]{2,1,0:T(8,128)(2,1)} %reduce-scatter.14.cloned.1.call-done) | copy-start | bytes 2359300
  351.2 94.0 %all-gather.17.cloned.1.call-start = ((), (), s32[]{:S(2)}) async-start(), calls=%async_computation.19 | async-start | bytes 3932160 | tf_op jit(solution)/shard_map/all_gather | solution.py:245
  401.2 146.4 %reduce-scatter.34.cloned.1.call-start = ((), (), s32[]{:S(2)}) async-start(), calls=%async_computation.27 | async-start | bytes 2359296
  458.7 2.3 copy-start.13
  461.7 2.7 copy-start.14
  469.6 2.3 copy-start.13
  472.7 2.7 copy-start.14
  480.6 2.3 copy-start.13
  483.6 2.7 copy-start.14
  491.6 2.3 copy-start.13
  494.6 2.7 copy-start.14
  503.9 1.1 copy-start.9
  503.9 72.5 %reduce-scatter.20.cloned.1.call-start = ((), (), s32[]{:S(2)}) async-start(), calls=%async_computation.20 | async-start | bytes 2359296 | tf_op jit(solution)/shard_map/reduce_scatter | solution.py:289
  504.5 106.2 %reduce-scatter.26.cloned.1.call-start = ((), (), s32[]{:S(2)}) async-start(), calls=%async_computation.23 | async-start | bytes 1327104 | tf_op jit(solution)/shard_map/reduce_scatter | solution.py:361
  509.8 178.6 %reduce-scatter.28.cloned.1.call-start = ((), (), s32[]{:S(2)}) async-start(), calls=%async_computation.24 | async-start | bytes 7962624 | tf_op jit(solution)/shard_map/reduce_scatter | solution.py:364
  522.2 244.1 %reduce-scatter.30.cloned.1.call-start = ((), (), s32[]{:S(2)}) async-start(), calls=%async_computation.25 | async-start | bytes 7962624 | tf_op jit(solution)/shard_map/reduce_scatter | solution.py:367
  535.0 309.1 %reduce-scatter.32.cloned.1.call-start = ((), (), s32[]{:S(2)}) async-start(), calls=%async_computation.26 | async-start | bytes 7962624 | tf_op jit(solution)/shard_map/reduce_scatter | solution.py:370
  547.4 1.4 copy-start.28
  547.4 1.4 copy-start.35
  547.4 2.6 copy-start.12
  547.5 330.4 %reduce-scatter.24.cloned.1.call-start = ((), (), s32[]{:S(2)}) async-start(), calls=%async_computation.22 | async-start | bytes 1327104 | tf_op jit(solution)/shard_map/reduce_scatter | solution.py:358
  548.8 3.8 copy-start.3
  550.1 47.5 %copy-start.15 = (bf16[8,128,64]{1,2,0:T(8,128)(2,1)}, bf16[8,128,64]{1,2,0:T(8,128)(2,1)S(1)}, u32[]{:S(2)}) copy-start(bf16[8,128,64]{1,2,0:T(8,128)(2,1)S(1)} %get-tuple-element.335) | copy-start | bytes 393220
  552.6 3.3 copy-start.18
  555.5 367.6 %reduce-scatter.22.cloned.1.call-start = ((), (), s32[]{:S(2)}) async-start(), calls=%async_computation.21 | async-start | bytes 3932160 | tf_op jit(solution)/shard_map/reduce_scatter | solution.py:313
  556.0 3.7 copy-start.20
  559.6 16.8 %copy-start.23 = (bf16[1536,128]{1,0:T(8,128)(2,1)S(1)}, bf16[1536,128]{1,0:T(8,128)(2,1)}, u32[]{:S(2)}) copy-start(bf16[1536,128]{1,0:T(8,128)(2,1)} %param.26) | copy-start | bytes 1179652
  583.8 386.9 %reduce-scatter.16.cloned.1.call-start = ((), (), s32[]{:S(2)}) async-start(), calls=%async_computation.16 | async-start | bytes 3932160 | tf_op jit(solution)/shard_map/reduce_scatter | solution.py:222
  596.2 518.6 %all-reduce.4.cloned.1.call-start = ((), (), s32[]{:S(2)}) async-start(), calls=%async_computation.28 | async-start | bytes 6291456 | tf_op jit(solution)/shard_map/psum | solution.py:345
  597.5 5.2 copy-start.4
  597.5 5.2 copy-start.10
  690.9 232.2 %copy-start.25 = (f32[1536]{0:T(1024)S(1)}, f32[1536]{0:T(1024)}, u32[]{:S(2)}) copy-start(f32[1536]{0:T(1024)} %copy-done.24) | copy-start | bytes 18436
  768.9 201.8 %copy-start.6 = (bf16[2,128,1536]{2,1,0:T(8,128)(2,1)S(1)}, bf16[2,128,1536]{2,1,0:T(8,128)(2,1)}, u32[]{:S(2)}) copy-start(bf16[2,128,1536]{2,1,0:T(8,128)(2,1)} %param.35) | copy-start | bytes 2359300
  768.9 201.8 %copy-start.7 = (bf16[2,128,1536]{2,1,0:T(8,128)(2,1)S(1)}, bf16[2,128,1536]{2,1,0:T(8,128)(2,1)}, u32[]{:S(2)}) copy-start(bf16[2,128,1536]{2,1,0:T(8,128)(2,1)} %reduce-scatter.18.cloned.1.call-done) | copy-start | bytes 2359300
  1114.8 2.8 copy-start.16
  1114.8 4.0 copy-start.1
  (1 other events, 0.5 us)
Sparse Core Ops, SparseCore 0:
  11.9 46.6 all-gather.6
  64.4 30.8 all-gather.10
  97.5 28.1 all-gather.8
  161.3 43.4 reduce-scatter.13
  206.5 43.9 all-gather.14
  252.8 43.9 all-gather.12
  351.4 43.9 reduce-scatter.17
  401.3 43.9 all-gather.16
  504.0 35.7 reduce-scatter.33
  542.0 34.4 reduce-scatter.19
  579.3 31.3 reduce-scatter.25
  612.9 75.4 reduce-scatter.27
  690.7 75.5 reduce-scatter.29
  768.5 75.5 reduce-scatter.31
  846.9 30.9 reduce-scatter.23
  880.7 42.3 reduce-scatter.21
  925.9 44.6 reduce-scatter.15
  976.7 138.0 all-reduce.3
where the time goes:
time: 1140 us; the launch traced here: 1130 us
  waiting for transfers between devices  758 us (66%)
  matrix products  219 us (19%)
  other arithmetic  53 us (5%)
  blocking collectives  40.6 us (4%)
  local copies, waits for them, and re-layouts  38.4 us (3%)
  between operations  15 us (1%)
    psum x1, waiting for transfers between devices, local(): lax.psum((gain_one_part, gain_two_part, query_bias_full, key_bias_full, v...  140 us
    reduce_scatter x2, waiting for transfers between devices, local(): lax.psum_scatter(normed_grad_part.astype(jnp.bfloat16), ('kv', 'qh'), sca...  87.7 us
    reduce_scatter x1, waiting for transfers between devices, local(): lax.psum_scatter(gate_grad.astype(jnp.bfloat16), 'seq', scatter_dimension...  76.1 us
    reduce_scatter x1, waiting for transfers between devices, local(): lax.psum_scatter(up_grad.astype(jnp.bfloat16), 'seq', scatter_dimension=0...  75.4 us
    reduce_scatter x1, waiting for transfers between devices, local(): lax.psum_scatter(down_grad.astype(jnp.bfloat16), 'seq', scatter_dimension...  75.3 us
    all_gather x1, waiting for transfers between devices, local(): lax.all_gather(normed_one.astype(jnp.bfloat16), ('kv', 'qh'), axis=0, til...  46.7 us
    all_gather x1, waiting for transfers between devices, local(): lax.all_gather(grad_hidden.astype(jnp.bfloat16), ('kv', 'qh'), axis=0, ti...  44 us
    reduce_scatter x1, waiting for transfers between devices, local(): lax.psum_scatter(branch.astype(jnp.bfloat16), ('kv', 'qh'), scatter_dimen...  42.9 us
  transfers between devices with their start and end apart: 18, of which 17 were waited for; matrix products, arithmetic and copies ran while one was open for 13% of the time, Pallas kernels for 0%

commit v1 on v0

v1 whole, which is shorter than its diff:
```python
import functools
import jax
import jax.numpy as jnp
from jax import lax
from jax.experimental import pallas as pl
from jax.experimental.pallas import tpu as pltpu
from jax.sharding import PartitionSpec as P

epsilon = 1e-06
rope_base = 1000000.0
MESH = pl.DeviceIdType.MESH
ANY = pl.BlockSpec(memory_space=pl.ANY)
VMEM = pl.BlockSpec(memory_space=pltpu.VMEM)
bf16 = jnp.bfloat16
f32 = jnp.float32


class Place:
    def __init__(self, seq_size):
        k, q, s = lax.axis_index("kv"), lax.axis_index("qh"), lax.axis_index("seq")
        self.kv, self.qh, self.seq = k, q, s
        self.chip, self.core = s // 2, lax.rem(s, 2)
        self.chips = seq_size // 2
        self.across_x = (1 - k, q, s)
        self.across_y = (k, 1 - q, s)
        self.diagonal = (1 - k, 1 - q, s)
        self.sibling = (k, q, s + 1 - 2 * self.core)
        self.above = (k, q, s + 2)
        self.below = (k, q, s - 2)
        self.has_above = self.chip < self.chips - 1
        self.has_below = self.chip > 0


class Wires:
    def __init__(self, send, recv, local):
        self.send, self.recv, self.local = send, recv, local
        self.count = self.local_count = 0

    def remote(self, src, dst, device):
        i = self.count
        self.count += 1
        return pltpu.make_async_remote_copy(
            src_ref=src,
            dst_ref=dst,
            send_sem=self.send.at[i],
            recv_sem=self.recv.at[i],
            device_id=device,
            device_id_type=MESH,
        )

    def copy(self, src, dst):
        i = self.local_count
        self.local_count += 1
        return pltpu.make_async_copy(src, dst, self.local.at[i])


def greet(devices, conditional):
    barrier = pltpu.get_barrier_semaphore()
    for device in devices:
        pl.semaphore_signal(barrier, inc=1, device_id=device, device_id_type=MESH)
    for present, device in conditional:

        @pl.when(present)
        def _(device=device):
            pl.semaphore_signal(barrier, inc=1, device_id=device, device_id_type=MESH)

    return barrier


def dot(a, b, dims=((1,), (0,))):
    return lax.dot_general(a, b, (dims, ((), ())), preferred_element_type=f32)


def turn(v, cosine, sine):
    return v * cosine + pltpu.roll(v, v.shape[-1] // 2, v.ndim - 1) * sine


class WeightGather:
    def __init__(self, place, wires, own, gathered):
        rows = own.shape[0]
        half, quarter = rows // 2, rows // 4
        self.place, self.gathered = place, gathered
        base = place.core * half
        mine = pl.ds(pl.multiple_of(base, half), half)
        first = pl.ds(pl.multiple_of(base, quarter), quarter)
        second = pl.ds(pl.multiple_of(base + quarter, quarter), quarter)
        g = gathered
        self.x = wires.remote(own.at[mine], g.at[0, mine], place.across_x)
        self.y = wires.remote(own.at[mine], g.at[1, mine], place.across_y)
        self.dx = wires.remote(g.at[1, first], g.at[2, first], place.across_x)
        self.dy = wires.remote(g.at[0, second], g.at[2, second], place.across_y)
        self.share = [
            wires.remote(g.at[0, mine], g.at[0, mine], place.sibling),
            wires.remote(g.at[1, mine], g.at[1, mine], place.sibling),
            wires.remote(g.at[2, first], g.at[2, first], place.sibling),
            wires.remote(g.at[2, second], g.at[2, second], place.sibling),
        ]

    def begin(self):
        self.x.start()
        self.y.start()

    def got_x(self):
        self.x.wait_recv()
        self.dy.start()
        self.share[0].start()

    def got_y(self):
        self.y.wait_recv()
        self.dx.start()
        self.share[1].start()

    def got_diagonal(self):
        self.dx.wait_recv()
        self.share[2].start()
        self.dy.wait_recv()
        self.share[3].start()

    def complete(self, block):
        for i in ((0,), (1,), (2, 3))[block]:
            self.share[i].wait_recv()

    def drain(self):
        for copy in [self.x, self.y, self.dx, self.dy] + self.share:
            copy.wait_send()


class TokenGather:
    def __init__(self, place, wires, own, gathered):
        half = own.shape[0] // 2
        g = gathered
        self.x = wires.remote(own, g.at[1], place.across_x)
        self.y = wires.remote(own, g.at[2], place.across_y)
        self.dx = wires.remote(g.at[2, pl.ds(0, half)], g.at[3, pl.ds(0, half)], place.across_x)
        self.dy = wires.remote(g.at[1, pl.ds(half, half)], g.at[3, pl.ds(half, half)], place.across_y)
        self.local = wires.copy(own, g.at[0])

    def begin(self):
        self.x.start()
        self.y.start()
        self.local.start()

    def relay(self):
        self.y.wait_recv()
        self.dx.start()
        self.x.wait_recv()
        self.dy.start()

    def finish(self):
        self.dx.wait_recv()
        self.dy.wait_recv()
        self.local.wait()
        for copy in (self.x, self.y, self.dx, self.dy):
            copy.wait_send()


def front_kernel(
    seq_size,
    tok_ref, cot_ref, gain_one_ref, gain_two_ref, wq_ref, wkv_ref, wo_ref, bias_ref, cos_ref, sin_ref, qseg_ref, kseg_ref,
    wqg_ref, wog_ref, wkvg_ref, x2g_ref, cotg_ref, hidden_ref, n1_ref, q_ref, kv_ref, p_ref, ctx_ref,
    biasg, wkv_v, wq_v, wo_v, n1_v, q_v, kv_v, ctx_v, hidden_v, x2_v, mask_v, p_v, send, recv, local,
):
    place = Place(seq_size)
    wires = Wires(send, recv, local)
    chips = place.chips
    tok = tok_ref.shape[0]
    span = tok // 2
    keys = kv_v.shape[2]

    kv_v[...] = jnp.zeros_like(kv_v)
    barrier = greet(
        [place.across_x, place.across_y, place.diagonal, place.sibling], [(place.has_below, place.below)]
    )
    pl.semaphore_wait(barrier, 4 + jnp.where(place.has_above, 1, 0))

    half = wkv_ref.shape[0] // 2
    mine = pl.ds(pl.multiple_of(place.core * half, half), half)
    kvx = wires.remote(wkv_ref.at[mine], wkvg_ref.at[mine], place.across_x)
    kvs = wires.remote(wkvg_ref.at[mine], wkvg_ref.at[mine], place.sibling)
    biases = [
        wires.remote(bias_ref, biasg.at[i], device)
        for i, device in enumerate((place.across_x, place.across_y, place.diagonal))
    ]
    gq = WeightGather(place, wires, wq_ref, wqg_ref)
    go = WeightGather(place, wires, wo_ref, wog_ref)
    kvx.start()
    for copy in biases:
        copy.start()
    gq.begin()

    load_kv = wires.copy(wkv_ref, wkv_v.at[0])
    load_q = wires.copy(wq_ref, wq_v.at[0])
    load_o = wires.copy(wo_ref, wo_v.at[0])
    for copy in (load_kv, load_q, load_o):
        copy.start()

    tokens = tok_ref[...].astype(f32)
    factor = lax.rsqrt(jnp.mean(tokens * tokens, axis=-1, keepdims=True) + epsilon)
    n1_v[...] = (tokens * factor * gain_one_ref[...]).astype(bf16)
    save_n1 = wires.copy(n1_v, n1_ref)
    save_n1.start()

    here = pl.ds(pl.multiple_of(place.seq * span, span), span)

    def project_kv(head, kbias, vbias):
        both = dot(n1_v[...], wkv_v[head])
        width = both.shape[1] // 2
        rotated = turn(both[:, :width] + kbias, cos_ref[...], sin_ref[...]).astype(bf16)
        kv_v[2 * head, :, here, :] = rotated.reshape(2, span, width)
        kv_v[2 * head + 1, :, here, :] = (both[:, width:] + vbias).astype(bf16).reshape(2, span, width)

    qw = wq_ref.shape[1]
    hd = cos_ref.shape[1]

    def biases_of(i):
        rows = bias_ref[0:1, :] if i == 0 else biasg[i - 1, 0:1, :]
        return rows[:, :qw], rows[:, qw : qw + hd], rows[:, qw + hd :]

    load_kv.wait()
    _, kb, vb = biases_of(0)
    project_kv(0, kb, vb)
    kvx.wait_recv()
    kvs.start()
    kvs.wait_recv()
    load_kvx = wires.copy(wkvg_ref, wkv_v.at[1])
    load_kvx.start()
    for copy in biases:
        copy.wait_recv()
    load_kvx.wait()
    _, kb, vb = biases_of(1)
    project_kv(1, kb, vb)

    def block(seq_index):
        return kv_v.at[:, :, pl.ds(pl.multiple_of(seq_index * span, span), span), :]

    ups = []
    shares = []
    for j in range(chips):
        ups.append(wires.remote(block(place.seq - 2 * j), block(place.seq - 2 * j), place.above) if j < chips - 1 else None)
        shares.append(wires.remote(block(place.seq - 2 * j), block(place.seq - 2 * j), place.sibling))

    def chain(j):
        @pl.when(place.chip >= j)
        def _():
            if j > 0:
                ups[j - 1].wait_recv()
            shares[j].start()
            if j < chips - 1:

                @pl.when(place.has_above)
                def _():
                    ups[j].start()

    chain(0)
    load_q.wait()

    def project_q(i):
        lin = dot(n1_v[...], wq_v[i]) + biases_of(i)[0]
        heads = qw // hd
        for h in range(heads):
            part = turn(lin[:, h * hd : (h + 1) * hd], cos_ref[...], sin_ref[...]).astype(bf16)
            q_v[i, 0, h] = part[:span]
            q_v[i, 1, h] = part[span:]

    project_q(0)
    gq.got_x()
    gq.got_y()
    go.begin()
    for j in range(1, (chips + 1) // 2):
        chain(j)
    for i in (1, 2):
        gq.complete(i - 1)
        load = wires.copy(wqg_ref.at[i - 1], wq_v.at[i])
        load.start()
        load.wait()
        project_q(i)
    gq.got_diagonal()
    for j in range((chips + 1) // 2, chips):
        chain(j)
    gq.complete(2)
    load = wires.copy(wqg_ref.at[2], wq_v.at[3])
    load.start()
    load.wait()
    project_q(3)
    save_q = wires.copy(q_v, q_ref)
    save_q.start()
    for j in range(chips):

        @pl.when(place.chip >= j)
        def _(j=j):
            shares[j].wait_recv()

    save_kv = wires.copy(kv_v, kv_ref)
    save_kv.start()

    gather_two = TokenGather(place, wires, x2_v, x2g_ref)
    gather_cot = TokenGather(place, wires, cot_ref, cotg_ref)
    scaling = hd ** (-0.5)
    heads = qw // hd
    key_order = lax.broadcasted_iota(jnp.int32, (span, keys), 1)
    query_order = lax.broadcasted_iota(jnp.int32, (span, keys), 0) + place.seq * span
    save_p = [[wires.copy(p_v.at[i], p_ref.at[r, i]) for i in range(4)] for r in range(2)]

    def attend(r):
        allowed = (key_order <= query_order) & (qseg_ref[r] == kseg_ref[r])
        mask_v[...] = jnp.where(allowed, 0.0, -1e30)

        def unit(i, carry):
            kvh = lax.rem(i, 2)
            queries = q_v[i, r].reshape(heads * span, hd)
            scores = dot(queries, kv_v[2 * kvh, r], ((1,), (1,))) * scaling
            scores = scores.reshape(heads, span, keys) + mask_v[...][None]
            row_max = jnp.max(scores, axis=-1, keepdims=True)
            exponent = jnp.exp(scores - row_max)
            total = jnp.sum(exponent, axis=-1, keepdims=True)
            probs = (exponent * (1.0 / total)).astype(bf16)
            p_v[i] = probs.reshape(heads * span, keys)
            context = dot(p_v[i], kv_v[2 * kvh + 1, r]).astype(bf16)
            for h in range(heads):
                ctx_v[i, r * span : (r + 1) * span, h * hd : (h + 1) * hd] = context[h * span : (h + 1) * span]
            return carry

        lax.fori_loop(0, 4, unit, 0)
        for copy in save_p[r]:
            copy.start()

    attend(0)
    go.got_x()
    go.got_y()
    gather_cot.begin()
    for copy in save_p[0]:
        copy.wait()
    attend(1)
    go.got_diagonal()
    save_ctx = wires.copy(ctx_v, ctx_ref)
    save_ctx.start()
    load_o.wait()
    hidden_v[...] = tok_ref[...].astype(f32) + dot(ctx_v[0], wo_v[0])
    for i in (1, 2, 3):
        go.complete(i - 1)
        load = wires.copy(wog_ref.at[i - 1], wo_v.at[i])
        load.start()
        load.wait()
        hidden_v[...] += dot(ctx_v[i], wo_v[i])
    save_hidden = wires.copy(hidden_v, hidden_ref)
    save_hidden.start()
    hidden = hidden_v[...]
    factor = lax.rsqrt(jnp.mean(hidden * hidden, axis=-1, keepdims=True) + epsilon)
    x2_v[...] = (hidden * factor * gain_two_ref[...]).astype(bf16)
    gather_two.begin()
    gather_cot.relay()
    gather_two.relay()

    for copy in save_p[1] + [save_n1, save_q, save_kv, save_ctx, save_hidden]:
        copy.wait()
    kvx.wait_send()
    kvs.wait_send()
    for copy in biases:
        copy.wait_send()
    gq.drain()
    go.drain()
    for j in range(chips):

        @pl.when(place.chip >= j)
        def _(j=j):
            shares[j].wait_send()
            if j < chips - 1:

                @pl.when(place.has_above)
                def _():
                    ups[j].wait_send()

    gather_cot.finish()
    gather_two.finish()


def front(seq_size, tok, cot, gain_one, gain_two, wq, wkv, wo, bias, cosine, sine, qseg, kseg):
    tokens, width = tok.shape
    span = tokens // 2
    qw, hd = wq.shape[1], cosine.shape[1]
    heads = qw // hd
    keys = kseg.shape[-1]
    chips = seq_size // 2
    shape = jax.ShapeDtypeStruct
    outs = (
        shape((3, width, qw), bf16),
        shape((3, qw, width), bf16),
        shape(wkv.shape, bf16),
        shape((4, tokens, width), bf16),
        shape((4, tokens, width), bf16),
        shape((tokens, width), f32),
        shape((tokens, width), bf16),
        shape((4, 2, heads, span, hd), bf16),
        shape((4, 2, keys, hd), bf16),
        shape((2, 4, heads * span, keys), bf16),
        shape((4, tokens, qw), bf16),
    )
    remotes = 5 + 8 + 8 + 2 * chips + 8
    scratch = [
        pltpu.VMEM((3,) + bias.shape, f32),
        pltpu.VMEM((2,) + wkv.shape, bf16),
        pltpu.VMEM((4, width, qw), bf16),
        pltpu.VMEM((4, qw, width), bf16),
        pltpu.VMEM((tokens, width), bf16),
        pltpu.VMEM((4, 2, heads, span, hd), bf16),
        pltpu.VMEM((4, 2, keys, hd), bf16),
        pltpu.VMEM((4, tokens, qw), bf16),
        pltpu.VMEM((tokens, width), f32),
        pltpu.VMEM((tokens, width), bf16),
        pltpu.VMEM((span, keys), f32),
        pltpu.VMEM((4, heads * span, keys), bf16),
        pltpu.SemaphoreType.DMA((remotes,)),
        pltpu.SemaphoreType.DMA((remotes,)),
        pltpu.SemaphoreType.DMA((32,)),
    ]
    return pl.pallas_call(
        functools.partial(front_kernel, seq_size),
        out_shape=outs,
        in_specs=[VMEM, ANY, VMEM, VMEM, ANY, ANY, ANY, VMEM, VMEM, VMEM, VMEM, VMEM],
        out_specs=tuple([ANY] * len(outs)),
        scratch_shapes=scratch,
        name="attention_front",
        compiler_params=pltpu.CompilerParams(
            collective_id=0, has_side_effects=True, vmem_limit_bytes=56 * 2**20
        ),
    )(tok, cot, gain_one, gain_two, wq, wkv, wo, bias, cosine, sine, qseg, kseg)


def rotate_rows(v, cosine, sine):
    half = v.shape[-1] // 2
    return v * cosine + jnp.concatenate([v[..., half:], v[..., :half]], -1) * sine


def swap(v, axis):
    return lax.ppermute(v, axis, [(0, 1), (1, 0)])


def sum_plane(parts):
    low = parts.astype(bf16)
    came = swap(jnp.stack([low[1], low[3]]), "kv").astype(f32)
    kept = parts[0].astype(f32) + came[0]
    passed = (parts[2].astype(f32) + came[1]).astype(bf16)
    return kept + swap(passed, "qh").astype(f32)


def normalize_back(vectors, gain, grad_in):
    inv = lax.rsqrt(jnp.mean(vectors * vectors, axis=-1, keepdims=True) + epsilon)
    weighted = grad_in * gain
    inner = jnp.mean(vectors * weighted, axis=-1, keepdims=True)
    back = inv * weighted - vectors * inv * inv * inv * inner
    return back, jnp.sum(grad_in * vectors * inv, axis=0)


def einsum(spec, a, b):
    return jnp.einsum(spec, a, b, preferred_element_type=f32)


def local(
    seq_size,
    tokens, attn_gain, query_weight, query_bias, key_matrix, key_offset_bias, value_matrix, value_offset_bias, out_weight,
    mlp_gain, gate_weight, up_weight, down_weight, segment_ids, position_ids, cotangent,
):
    rows, span, width = tokens.shape
    count = rows * span
    hd = key_matrix.shape[1]
    qw = query_weight.shape[1]
    heads = qw // hd
    k, q, s = lax.axis_index("kv"), lax.axis_index("qh"), lax.axis_index("seq")
    row_start = (2 * k + q) * rows
    gain_one = attn_gain.astype(f32)[None]
    gain_two = mlp_gain.astype(f32)[None]
    positions = lax.dynamic_slice_in_dim(position_ids, row_start, rows, 0)
    inverse = 1.0 / jnp.power(rope_base, jnp.arange(hd // 2, dtype=f32) * 2.0 / hd)
    phase = positions.astype(f32).reshape(count, 1) * inverse
    cosine, sine = jnp.cos(phase), jnp.sin(phase)
    cosine = jnp.concatenate([cosine, cosine], -1)
    sine = jnp.concatenate([-sine, sine], -1)
    segs = lax.dynamic_slice_in_dim(segment_ids, row_start, rows, 0)
    qseg = lax.dynamic_slice_in_dim(segs, s * span, span, 1)[:, :, None]
    kseg = segs[:, None, :]
    tok = tokens.reshape(count, width)
    cot = cotangent.reshape(count, width)
    wkv = jnp.concatenate([key_matrix, value_matrix], 1)
    bias = jnp.concatenate([query_bias, key_offset_bias, value_offset_bias]).astype(f32)
    bias = jnp.broadcast_to(bias[None], (8, bias.shape[0]))
    wqg, wog, wkvg, x2g, cotg, hidden, n1, qrot, kv, probs, ctx = front(
        seq_size, tok, cot, gain_one, gain_two, query_weight, wkv, out_weight, bias, cosine, sine, qseg, kseg
    )
    x2 = x2g.reshape(4 * count, width)
    cots = cotg.reshape(4 * count, width)
    gate = jnp.dot(x2, gate_weight, preferred_element_type=f32)
    up = jnp.dot(x2, up_weight, preferred_element_type=f32)
    sig = jax.nn.sigmoid(gate)
    silu = gate * sig
    activation = (silu * up).astype(bf16)
    grad_act = einsum("td,fd->tf", cots, down_weight)
    grad_gate = (grad_act * up * sig * (1.0 + gate * (1.0 - sig))).astype(bf16)
    grad_up = (grad_act * silu).astype(bf16)
    down_grad = einsum("tf,td->fd", activation, cots).astype(bf16)
    gate_grad = einsum("td,tf->df", x2, grad_gate).astype(bf16)
    up_grad = einsum("td,tf->df", x2, grad_up).astype(bf16)
    normed_part = einsum("tf,df->td", grad_gate, gate_weight) + einsum("tf,df->td", grad_up, up_weight)
    normed_grad = sum_plane(normed_part.astype(bf16).reshape(4, count, width))
    back, gain_two_part = normalize_back(hidden, gain_two, normed_grad)
    grad_hidden = cot.astype(f32) + back
    branch = grad_hidden.astype(bf16)
    mlp_part = jnp.dot(activation, down_weight, preferred_element_type=f32)
    output = (hidden + sum_plane(mlp_part.astype(bf16).reshape(4, count, width))).astype(bf16)

    wo_all = jnp.concatenate([out_weight[None], wog])
    wq_all = jnp.concatenate([query_weight[None], wqg])
    wkv_all = jnp.stack([wkv, wkvg])
    out_grad = einsum("btc,td->bcd", ctx, branch).astype(bf16)
    grad_ctx = einsum("td,bcd->btc", branch, wo_all)
    inner = jnp.sum((grad_ctx * ctx.astype(f32)).reshape(4, rows, span, heads, hd), -1)
    grad_ctx = grad_ctx.astype(bf16).reshape(4, rows, span, heads, hd).transpose(0, 1, 3, 2, 4)
    inner = inner.transpose(0, 1, 3, 2)[..., None]
    keys = kv.shape[2]
    pr = probs.reshape(rows, 4, heads, span, keys).transpose(1, 0, 2, 3, 4)
    scaling = hd ** (-0.5)

    def by_head(v):
        return v.reshape((2, 2) + v.shape[1:])

    pr, qh, gc, inner = by_head(pr), by_head(qrot), by_head(grad_ctx), by_head(inner)
    kvs = kv.reshape((2, 2) + kv.shape[1:])
    grad_probs = einsum("bgrhqd,grkd->bgrhqk", gc, kvs[:, 1])
    grad_scores = (pr.astype(f32) * (grad_probs - inner)).astype(bf16)
    grad_q = einsum("bgrhqk,grkd->bgrhqd", grad_scores, kvs[:, 0]) * scaling
    grad_k = einsum("bgrhqk,bgrhqd->grkd", grad_scores, qh) * scaling
    grad_v = einsum("bgrhqk,bgrhqd->grkd", pr, gc)
    grad_kv = lax.psum_scatter(
        jnp.stack([grad_k, grad_v]).astype(bf16), "seq", scatter_dimension=3, tiled=True
    ).astype(f32)
    grad_kv = grad_kv.reshape(2, 2, count, hd)
    gk = rotate_rows(grad_kv[0], cosine, -sine).astype(bf16)
    gv = grad_kv[1].astype(bf16)
    gq = grad_q.reshape(4, rows, heads, span, hd)
    gq = rotate_rows(gq, cosine.reshape(rows, 1, span, hd), -sine.reshape(rows, 1, span, hd)).astype(bf16)
    gq = gq.transpose(0, 1, 3, 2, 4).reshape(4, count, qw)
    query_grad = einsum("td,btc->bdc", n1, gq).astype(bf16)
    gkv = jnp.concatenate([gk, gv], -1)
    kv_grad = einsum("td,gtc->gdc", n1, gkv).astype(bf16)
    normed_grad_one = einsum("btc,bdc->td", gq, wq_all) + einsum("gtc,gdc->td", gkv, wkv_all)
    back, gain_one_part = normalize_back(tok.astype(f32), gain_one, normed_grad_one)
    tokens_grad = grad_hidden + back

    query_out = lax.psum_scatter(
        sum_plane(query_grad).astype(bf16), "seq", scatter_dimension=0, tiled=True
    ).astype(f32)
    out_out = lax.psum_scatter(sum_plane(out_grad).astype(bf16), "seq", scatter_dimension=1, tiled=True).astype(f32)
    kv_sum = (kv_grad[0].astype(f32) + swap(kv_grad[1], "kv").astype(f32)).astype(bf16)
    kv_sum = lax.psum_scatter(kv_sum, ("qh", "seq"), scatter_dimension=0, tiled=True)
    kv_sum = lax.all_gather(kv_sum, ("qh", "seq"), axis=0, tiled=True)
    kv_sum = lax.all_gather(kv_sum, "kv", axis=0).astype(f32)
    key_out = jnp.concatenate([kv_sum[0, :, :hd], kv_sum[1, :, :hd]], 1)
    value_out = jnp.concatenate([kv_sum[0, :, hd:], kv_sum[1, :, hd:]], 1)

    blocks = [2 * k + q, 2 * (1 - k) + q, 2 * k + 1 - q, 2 * (1 - k) + 1 - q]
    bq = jnp.zeros((4, qw), f32)
    sums = jnp.sum(gq.astype(f32), axis=1)
    for i in range(4):
        bq = lax.dynamic_update_slice(bq, sums[i : i + 1], (blocks[i], 0))
    bkv = jnp.sum(gkv.astype(f32), axis=1)
    bkv = lax.select(jnp.broadcast_to(k == 0, bkv.shape), bkv, bkv[::-1])
    packed = jnp.concatenate([gain_one_part, gain_two_part, bq.reshape(-1), bkv.reshape(-1)])
    packed = lax.psum(packed, ("kv", "qh", "seq"))
    n = width
    m = 4 * qw
    bkv = packed[2 * n + m :].reshape(2, 2, hd)

    def scatter(v, dim):
        return lax.psum_scatter(v, "seq", scatter_dimension=dim, tiled=True).astype(f32)

    return (
        output.reshape(tokens.shape),
        tokens_grad.reshape(tokens.shape),
        packed[:n],
        query_out,
        packed[2 * n : 2 * n + m],
        key_out,
        bkv[:, 0].reshape(-1),
        value_out,
        bkv[:, 1].reshape(-1),
        out_out,
        packed[n : 2 * n],
        scatter(gate_grad, 0),
        scatter(up_grad, 0),
        scatter(down_grad, 1),
    )


def solution(mesh):
    return jax.shard_map(
        functools.partial(local, mesh.shape["seq"]),
        mesh=mesh,
        in_specs=(
            P(("kv", "qh"), "seq", None),
            P(),
            P(None, ("kv", "qh")),
            P(("kv", "qh")),
            P(None, "kv"),
            P("kv"),
            P(None, "kv"),
            P("kv"),
            P(("kv", "qh"), None),
            P(),
            P(None, ("kv", "qh")),
            P(None, ("kv", "qh")),
            P(("kv", "qh"), None),
            P(),
            P(None, "seq"),
            P(("kv", "qh"), "seq", None),
        ),
        out_specs=(
            P(("kv", "qh"), "seq", None),
            P(("kv", "qh"), "seq", None),
            P(),
            P("seq", ("kv", "qh")),
            P(),
            P(),
            P(),
            P(),
            P(),
            P(("kv", "qh"), "seq"),
            P(),
            P("seq", ("kv", "qh")),
            P("seq", ("kv", "qh")),
            P(("kv", "qh"), "seq"),
        ),
        check_vma=False,
    )
```

time: 1140 us -> 840 us (0.74)
  waiting for transfers between devices: 758 us -> 391 us
  Pallas kernels: 0 us -> 108 us
  matrix products: 219 us -> 134 us
  blocking collectives: 40.6 us -> 66.1 us
  local copies, waits for them, and re-layouts: 38.4 us -> 52.4 us
  starting transfers between devices: 1.61 us -> 13.8 us
    all_gather x6 -> x1, waiting for transfers between devices: 208 us -> 0.01 us  [local(): kv_sum = lax.all_gather(kv_sum, 'kv', axis=0).astype(f32)]
    reduce_scatter x10 -> x5, waiting for transfers between devices: 409 us -> 238 us  [the longest x3 204 us: scatter(): lax.psum_scatter(v, 'seq', scatter_dimension=dim, tiled=True).astype(f32)]
    ppermute x0 -> x9, waiting for transfers between devices: none -> 153 us  [swap(): return lax.ppermute(v, axis, [(0, 1), (1, 0)])]
    psum x1 -> x0, waiting for transfers between devices: 140 us -> none  [local(): lax.psum((gain_one_part, gain_two_part, query_bias_full, key_bias_full, v...]
    pallas_call x0 -> x1, Pallas kernels: none -> 108 us  [front(): pl.pallas_call(functools.partial(front_kernel, seq_size), out_shape=outs,...]
    dot_general x49 -> x19, matrix products: 219 us -> 134 us  [the longest x16 104 us: einsum(): return jnp.einsum(spec, a, b, preferred_element_type=f32)]
    all_gather x0 -> x1, blocking collectives: none -> 27.5 us  [local(): kv_sum = lax.all_gather(kv_sum, ('qh', 'seq'), axis=0, tiled=True)]
    ppermute x0 -> x9, starting transfers between devices: none -> 12.9 us  [swap(): return lax.ppermute(v, axis, [(0, 1), (1, 0)])]
  transfers between devices with their start and end apart: 18 -> 17, of which waited for: 17 -> 11; matrix products, arithmetic and copies ran while one was open for 13% -> 15% of each run, Pallas kernels for 0% -> 0%
where the time goes in v1:
time: 840 us; the launch traced here: 835 us
  waiting for transfers between devices  391 us (47%)
  matrix products  134 us (16%)
  Pallas kernels  108 us (13%)
  blocking collectives  66.1 us (8%)
  other arithmetic  53 us (6%)
  local copies, waits for them, and re-layouts  52.4 us (6%)
  between operations  15.4 us (2%)
  starting transfers between devices  13.8 us (2%)
    reduce_scatter x3, waiting for transfers between devices, scatter(): lax.psum_scatter(v, 'seq', scatter_dimension=dim, tiled=True).astype(f32)  204 us
    ppermute x9, waiting for transfers between devices, swap(): return lax.ppermute(v, axis, [(0, 1), (1, 0)])  153 us
    pallas_call x1, Pallas kernels, front(): pl.pallas_call(functools.partial(front_kernel, seq_size), out_shape=outs,...  108 us
    dot_general x16, matrix products, einsum(): return jnp.einsum(spec, a, b, preferred_element_type=f32)  104 us
    psum x1, blocking collectives, local(): packed = lax.psum(packed, ('kv', 'qh', 'seq'))  38.5 us
    all_gather x1, blocking collectives, local(): kv_sum = lax.all_gather(kv_sum, ('qh', 'seq'), axis=0, tiled=True)  27.5 us
    reduce_scatter x1, waiting for transfers between devices, local(): lax.psum_scatter(kv_sum, ('qh', 'seq'), scatter_dimension=0, tiled=True)  22 us
    unnamed x114, local copies, waits for them, and re-layouts  20.1 us
  transfers between devices with their start and end apart: 17, of which 11 were waited for; matrix products, arithmetic and copies ran while one was open for 15% of the time, Pallas kernels for 0%

profile of v1, /device:TPU:0, one launch (start us, length us, event | category | flops | bytes accessed | tf_op | source)
XLA Modules:
  0.0 834.6 jit_solution(14253724356011867257)
XLA Ops:
  16.4 108.2 %attention_front.1 = (bf16[3,1536,384]{2,1,0:T(8,128)(2,1)}, bf16[3,384,1536]{2,1,0:T(8,128)(2,1)}, bf16[1536,256]{1,0:T(8,128)(2,1)}, bf16[4,256,1536]{2,1,0:T(...) custom-call(bf16[256,1536]{1,0:T(8,128)(2,1)} %bitcast.252, ...), custom_call_target="tpu_custom_call" | custom-call | tf_op jit(solution)/shard_map/attention_front/pallas_call | solution.py:416
  124.6 12.8 %fusion.84 = f32[1024,2240]{0,1:T(8,128)} fusion(bf16[1024,1536]{1,0:T(8,128)(2,1)} %bitcast.290, bf16[1536,2240]{0,1:T(8,128)(2,1)} %param.26), kind=kOutput, calls=%fused_computation.168 | convolution fusion | flops 7046430720 | bytes 19202048 | tf_op jit(solution)/shard_map/dot_general | solution.py:491
  137.4 9.8 %fusion.85 = f32[1024,2240]{0,1:T(8,128)} fusion(bf16[1024,1536]{1,0:T(8,128)(2,1)S(1)} %bitcast.293, bf16[1536,2240]{0,1:T(8,128)(2,1)S(1)} %bitcast.285), kind=kOutput, calls=%fused_computation.169 | convolution fusion | flops 7046430720 | bytes 19202048 | tf_op jit(solution)/shard_map/dot_general | solution.py:492
  147.2 20.4 %multiply_convert_fusion = (bf16[1024,2240]{0,1:T(8,128)(2,1)}, bf16[1024,2240]{0,1:T(8,128)(2,1)}, bf16[1024,2240]{0,1:T(8,128)(2,1)}) fusion(f32[1024,2240]{0,1:T(8,128)} %fusion.84, f32[1024,2240]{0,1:T(8,128)} %fusion.85, bf16[1024,1536]{1,0:T(8,128)(2,1)S(1)} %bitcast.289, bf16[2240,1536]{1,0:T(8,128)(2,1)} %param.28), kind=kOutput, calls=%fused_computation.6 | convolution fusion | flops 7080837120 | bytes 42139648 | tf_op jit(solution)/shard_map/td,fd->tf/dot_general | solution.py:455
  167.6 11.7 %fusion.86 = f32[1024,1536]{1,0:T(8,128)S(1)} fusion(bf16[1024,2240]{0,1:T(8,128)(2,1)} %get-tuple-element.101, bf16[1536,2240]{0,1:T(8,128)(2,1)} %param.26), kind=kOutput, calls=%fused_computation.170 | convolution fusion | flops 7046430720 | bytes 17760256 | tf_op jit(solution)/shard_map/tf,df->td/dot_general | solution.py:455
  179.4 10.7 %add_convert_fusion = bf16[1024,1536]{1,0:T(8,128)(2,1)S(1)} fusion(f32[1024,1536]{1,0:T(8,128)S(1)} %fusion.86, bf16[1024,2240]{0,1:T(8,128)(2,1)S(1)} %copy-done.39, bf16[1536,2240]{0,1:T(8,128)(2,1)} %param.27), kind=kOutput, calls=%fused_computation.13 | convolution fusion | flops 7049576448 | bytes 20905984 | tf_op jit(solution)/shard_map/tf,df->td/dot_general | solution.py:455
  190.4 1.6 collective-permute-start.2
  192.0 8.2 convolution_convert_fusion.4
  204.2 23.6 %collective-permute-done.2 = bf16[2,256,1536]{2,1,0:T(8,128)(2,1)S(1)} collective-permute-done((bf16[2,256,1536]{2,1,0:T(8,128)(2,1)S(1)}, bf16[2,256,1536]{2,1,0:T(8,128)(2,1)S(1)}, u32[]{:S(2)}, u32[]{:S(2)}) %collective-permute-start.2) | collective-permute-done | bytes 1572896 | tf_op jit(solution)/shard_map/ppermute | solution.py:435
  229.3 1.5 collective-permute-start.3
  231.0 9.0 %copy.99 = bf16[2,2,2,3,128,1024]{4,5,3,0,2,1:T(8,128)(2,1)} copy(bf16[2,2,2,3,128,1024]{5,4,3,1,0,2:T(8,128)(2,1)} %bitcast.253) | data formatting | bytes 12582912 | tf_op jit(solution)/shard_map/reshape | solution.py:523
  240.1 19.0 %collective-permute-done = bf16[2,256,1536]{2,1,0:T(8,128)(2,1)} collective-permute-done((bf16[2,256,1536]{2,1,0:T(8,128)(2,1)}, bf16[2,256,1536]{2,1,0:T(8,128)(2,1)}, u32[]{:S(2)}, u32[]{:S(2)}) %collective-permute-start) | collective-permute-done | bytes 1572896 | tf_op jit(solution)/shard_map/ppermute | solution.py:435
  259.0 2.0 convert_element_type.214
  261.2 1.6 collective-permute-start.1
  262.8 1.8 multiply_reduce_fusion
  264.7 13.6 %collective-permute-done.1 = bf16[256,1536]{1,0:T(8,128)(2,1)S(1)} collective-permute-done((bf16[256,1536]{1,0:T(8,128)(2,1)S(1)}, bf16[256,1536]{1,0:T(8,128)(2,1)S(1)}, u32[]{:S(2)}, u32[]{:S(2)}) %collective-permute-start.1) | collective-permute-done | bytes 786464 | tf_op jit(solution)/shard_map/ppermute | solution.py:435
  278.2 3.2 subtract_add_fusion
  281.4 2.3 bitcast_convert_fusion.1
  288.1 2.4 copy.103
  290.6 5.2 fusion.3
  295.9 1.5 copy-done.23
  297.4 1.8 fusion.1
  299.2 1.8 fusion.53
  301.8 1.5 pad_maximum_fusion.2
  306.6 2.2 copy-done.3
  308.8 1.7 pad_maximum_fusion.1
  310.5 1.5 collective-permute-start.7
  312.0 2.2 multiply_bitcast_fusion
  314.2 1.9 copy.108
  316.7 1.6 convert_reduce_fusion
  318.2 3.1 copy.109
  321.4 2.4 reshape.311
  325.4 2.0 copy-done.4
  327.4 1.6 pad_maximum_fusion
  330.5 12.1 %reduce-scatter.14.cloned.1.call-done = bf16[2,2,2,128,128]{4,3,2,1,0:T(8,128)(2,1)} async-done(((bf16[2,2,2,1024,128]{4,3,2,1,0:T(8,128)(2,1)}), bf16[2,2,2,128,128]{4,3,2,1,0:T(8,128)(2,1)}) %reduce-scatter.14.cloned.1.call-update) | async-done | bytes 262160 | tf_op jit(solution)/shard_map/reduce_scatter | solution.py:532
  344.5 1.5 collective-permute-start.6
  346.1 18.9 %collective-permute-done.7 = bf16[2,384,1536]{2,1,0:T(8,128)(2,1)} collective-permute-done((bf16[2,384,1536]{2,1,0:T(8,128)(2,1)}, bf16[2,384,1536]{2,1,0:T(8,128)(2,1)}, u32[]{:S(2)}, u32[]{:S(2)}) %collective-permute-start.7) | collective-permute-done | bytes 2359328 | tf_op jit(solution)/shard_map/ppermute | solution.py:435
  365.0 2.3 convert_element_type.259
  367.3 2.1 copy-done.5
  369.4 2.7 fusion.55
  372.1 1.5 collective-permute-start.8
  373.6 54.3 %collective-permute-done.6 = bf16[1536,256]{0,1:T(8,128)(2,1)S(1)} collective-permute-done((bf16[1536,256]{0,1:T(8,128)(2,1)S(1)}, bf16[1536,256]{0,1:T(8,128)(2,1)S(1)}, u32[]{:S(2)}, u32[]{:S(2)}) %collective-permute-start.6) | collective-permute-done | bytes 786464 | tf_op jit(solution)/shard_map/ppermute | solution.py:435
  429.3 4.6 convert_element_type.243
  433.9 2.2 fusion.23
  437.8 2.5 fusion.54
  440.3 1.6 collective-permute-start.5
  442.0 24.1 %collective-permute-done.5 = bf16[1536,384]{0,1:T(8,128)(2,1)S(1)} collective-permute-done((bf16[1536,384]{0,1:T(8,128)(2,1)S(1)}, bf16[1536,384]{0,1:T(8,128)(2,1)S(1)}, u32[]{:S(2)}, u32[]{:S(2)}) %collective-permute-start.5) | collective-permute-done | bytes 1179680 | tf_op jit(solution)/shard_map/ppermute | solution.py:435
  466.0 1.8 fusion.27
  469.3 22.0 %reduce-scatter.24.cloned.1.call-done = bf16[96,256]{1,0:T(8,128)(2,1)} async-done(((bf16[1536,256]{1,0:T(8,128)(2,1)}), bf16[96,256]{1,0:T(8,128)(2,1)}) %reduce-scatter.24.cloned.1.call-update) | async-done | bytes 49168 | tf_op jit(solution)/shard_map/reduce_scatter | solution.py:553
  491.3 27.5 %all_gather.9 = bf16[1536,256]{1,0:T(8,128)(2,1)} all-gather(bf16[96,256]{1,0:T(8,128)(2,1)} %reduce-scatter.24.cloned.1.call-done), channel_id=1, replica_groups=mesh['kv'=2,'qh'=2,'seq'=8] {'qh','seq'}, dimensions={0}, use_global_device_ids=true | all-gather | bytes 835584 | tf_op jit(solution)/shard_map/all_gather | solution.py:554
  518.9 12.3 %convolution_convert_fusion.2 = bf16[1536,2240]{1,0:T(8,128)(2,1)} fusion(bf16[1024,1536]{1,0:T(8,128)(2,1)} %bitcast.291, bf16[1024,2240]{0,1:T(8,128)(2,1)} %get-tuple-element.101), kind=kOutput, calls=%fused_computation.5 | convolution fusion | flops 7049871360 | bytes 14614528 | tf_op jit(solution)/shard_map/td,tf->df/dot_general | solution.py:455
  531.3 12.4 %convolution_convert_fusion.1 = bf16[1536,2240]{1,0:T(8,128)(2,1)} fusion(bf16[1024,1536]{1,0:T(8,128)(2,1)} %bitcast.292, bf16[1024,2240]{0,1:T(8,128)(2,1)} %get-tuple-element.100), kind=kOutput, calls=%fused_computation.4 | convolution fusion | flops 7049871360 | bytes 14614528 | tf_op jit(solution)/shard_map/td,tf->df/dot_general | solution.py:455
  544.1 12.4 %convolution_convert_fusion = bf16[2240,1536]{0,1:T(8,128)(2,1)} fusion(bf16[1024,2240]{0,1:T(8,128)(2,1)} %get-tuple-element.102, bf16[1024,1536]{1,0:T(8,128)(2,1)} %bitcast.288), kind=kOutput, calls=%fused_computation.3 | convolution fusion | flops 7049871360 | bytes 14614528 | tf_op jit(solution)/shard_map/tf,td->fd/dot_general | solution.py:455
  558.3 2.1 convolution_bitcast_fusion
  560.4 5.0 fusion.36
  565.4 38.5 %psum.7 = f32[5120]{0:T(1024)S(1)} all-reduce(f32[5120]{0:T(1024)S(1)} %pad_maximum_fusion.12), channel_id=1, replica_groups=mesh['kv'=2,'qh'=2,'seq'=8] {'kv','qh','seq'}, use_global_device_ids=true, to_apply=%region_10.0 | all-reduce | flops 5120 | bytes 40960 | tf_op jit(solution)/shard_map/psum | solution.py:567
  605.1 3.1 fusion.33
  612.0 1.7 convert.15
  616.3 52.5 %reduce-scatter.16.cloned.1.call-done = bf16[192,2240]{1,0:T(8,128)(2,1)} async-done(((bf16[1536,2240]{1,0:T(8,128)(2,1)}), bf16[192,2240]{1,0:T(8,128)(2,1)}) %reduce-scatter.16.cloned.1.call-update) | async-done | bytes 860176 | tf_op jit(solution)/shard_map/reduce_scatter | solution.py:573
  668.9 2.5 convert_element_type.267
  671.4 75.5 %reduce-scatter.18.cloned.1.call-done = bf16[192,2240]{1,0:T(8,128)(2,1)} async-done(((bf16[1536,2240]{1,0:T(8,128)(2,1)}), bf16[192,2240]{1,0:T(8,128)(2,1)}) %reduce-scatter.18.cloned.1.call-update) | async-done | bytes 860176 | tf_op jit(solution)/shard_map/reduce_scatter | solution.py:573
  746.9 2.5 convert_element_type.269
  749.4 75.6 %reduce-scatter.20.cloned.1.call-done = bf16[2240,192]{0,1:T(8,128)(2,1)} async-done(((bf16[2240,1536]{0,1:T(8,128)(2,1)}), bf16[2240,192]{0,1:T(8,128)(2,1)}) %reduce-scatter.20.cloned.1.call-update) | async-done | bytes 860176 | tf_op jit(solution)/shard_map/reduce_scatter | solution.py:573
  825.0 2.5 convert_element_type.271
  (207 shorter events, 43.5 us)
Async XLA Ops:
  7.2 8.6 %copy-start.32 = (bf16[384]{0:T(512)(128)(2,1)S(1)}, bf16[384]{0:T(512)(128)(2,1)}, u32[]{:S(2)}) copy-start(bf16[384]{0:T(512)(128)(2,1)} %param.19) | copy-start | bytes 2308
  7.2 8.6 %copy-start.34 = (bf16[128]{0:T(256)(128)(2,1)S(1)}, bf16[128]{0:T(256)(128)(2,1)}, u32[]{:S(2)}) copy-start(bf16[128]{0:T(256)(128)(2,1)} %param.21) | copy-start | bytes 772
  7.2 8.6 %copy-start.33 = (bf16[128]{0:T(256)(128)(2,1)S(1)}, bf16[128]{0:T(256)(128)(2,1)}, u32[]{:S(2)}) copy-start(bf16[128]{0:T(256)(128)(2,1)} %param.23) | copy-start | bytes 772
  7.2 335.4 %reduce-scatter.14.cloned.1.call-start = ((), (), s32[]{:S(2)}) async-start(), calls=%async_computation.7 | async-start | bytes 2359296 | tf_op jit(solution)/shard_map/reduce_scatter | solution.py:532
  14.8 1.6 copy-start.25
  16.4 121.0 %slice-start.4 = ((s8[6881280]{0:T(1024)(128)(4,1)}), s8[2686976]{0:T(1024)(128)(4,1)S(1)}, s32[]{:S(2)}) async-start(s8[6881280]{0:T(1024)(128)(4,1)} %bitcast.284), calls=%async_computation.19 | async-start | bytes 5373952
  124.6 12.8 %slice-start.5 = ((s8[6881280]{0:T(1024)(128)(4,1)}), s8[4194304]{0:T(1024)(128)(4,1)S(1)}, s32[]{:S(2)}) async-start(s8[6881280]{0:T(1024)(128)(4,1)} %bitcast.284), calls=%async_computation.20 | async-start | bytes 8388608
  124.6 12.8 %copy-start.37 = (bf16[4,256,1536]{2,1,0:T(8,128)(2,1)S(1)}, bf16[4,256,1536]{2,1,0:T(8,128)(2,1)}, u32[]{:S(2)}) copy-start(bf16[4,256,1536]{2,1,0:T(8,128)(2,1)} %get-tuple-element.26) | copy-start | bytes 9437188
  137.4 9.8 %copy-start.36 = (bf16[4,256,1536]{2,1,0:T(8,128)(2,1)S(1)}, bf16[4,256,1536]{2,1,0:T(8,128)(2,1)}, u32[]{:S(2)}) copy-start(bf16[4,256,1536]{2,1,0:T(8,128)(2,1)} %get-tuple-element.27) | copy-start | bytes 9437188
  167.6 11.8 %copy-start.39 = (bf16[1024,2240]{0,1:T(8,128)(2,1)S(1)}, bf16[1024,2240]{0,1:T(8,128)(2,1)}, u32[]{:S(2)}) copy-start(bf16[1024,2240]{0,1:T(8,128)(2,1)} %get-tuple-element.100) | copy-start | bytes 13762564
  167.6 24.4 %slice-start.6 = ((s8[6881280]{0:T(1024)(128)(4,1)}), s8[4194304]{0:T(1024)(128)(4,1)S(1)}, s32[]{:S(2)}) async-start(s8[6881280]{0:T(1024)(128)(4,1)} %bitcast.286), calls=%async_computation.21 | async-start | bytes 8388608
  167.6 24.4 %slice-start.8 = ((s8[4587520]{0:T(1024)(128)(4,1)}), s8[4194304]{0:T(1024)(128)(4,1)S(1)}, s32[]{:S(2)}) async-start(s8[4587520]{0:T(1024)(128)(4,1)} %bitcast.296), calls=%async_computation.23 | async-start | bytes 8388608
  179.3 12.6 %slice-start.7 = ((s8[6881280]{0:T(1024)(128)(4,1)}), s8[2686976]{0:T(1024)(128)(4,1)S(1)}, s32[]{:S(2)}) async-start(s8[6881280]{0:T(1024)(128)(4,1)} %bitcast.286), calls=%async_computation.22 | async-start | bytes 5373952
  179.4 12.6 %slice-start.9 = ((s8[4587520]{0:T(1024)(128)(4,1)}), s8[393216]{0:T(1024)(128)(4,1)S(1)}, s32[]{:S(2)}) async-start(s8[4587520]{0:T(1024)(128)(4,1)} %bitcast.296), calls=%async_computation.24 | async-start | bytes 786432
  190.1 38.1 %copy-start.13 = (bf16[1024,1536]{1,0:T(8,128)(2,1)}, bf16[1024,1536]{1,0:T(8,128)(2,1)S(1)}, u32[]{:S(2)}) copy-start(bf16[1024,1536]{1,0:T(8,128)(2,1)S(1)} %add_convert_fusion) | copy-start | bytes 9437188
  190.4 37.4 %collective-permute-start.2 = (bf16[2,256,1536]{2,1,0:T(8,128)(2,1)S(1)}, bf16[2,256,1536]{2,1,0:T(8,128)(2,1)S(1)}, u32[]{:S(2)}, u32[]{:S(2)}) collective-permute-start(bf16[2,256,1536]{2,1,0:T(8,128)(2,1)S(1)} %pad_maximum_fusion.4), channel_id=1, source_target_pairs={{0,16},{16,0},{1,17},{17,1},{2,18},{18,2},{3,19},{19,3},{4,20},{20... | collective-permute-start | bytes 4718600 | tf_op jit(solution)/shard_map/ppermute | solution.py:435
  200.2 2.2 copy-start.20
  202.4 56.6 %collective-permute-start = (bf16[2,256,1536]{2,1,0:T(8,128)(2,1)}, bf16[2,256,1536]{2,1,0:T(8,128)(2,1)}, u32[]{:S(2)}, u32[]{:S(2)}) collective-permute-start(bf16[2,256,1536]{2,1,0:T(8,128)(2,1)} %pad_maximum_fusion.3), channel_id=1, source_target_pairs={{0,16},{16,0},{1,17},{17,1},{2,18},{18,2},{3,19},{19,3},{4,20},{20... | collective-permute-start | bytes 4718600 | tf_op jit(solution)/shard_map/ppermute | solution.py:435
  228.2 2.6 copy-start.10
  228.2 2.8 copy-start.30
  229.3 33.5 %collective-permute-start.3 = (bf16[256,1536]{1,0:T(8,128)(2,1)}, bf16[256,1536]{1,0:T(8,128)(2,1)}, u32[]{:S(2)}, u32[]{:S(2)}) collective-permute-start(bf16[256,1536]{1,0:T(8,128)(2,1)} %fusion.38), channel_id=1, source_target_pairs={{0,8},{8,0},{1,9},{9,1},{2,10},{10,2},{3,11},{11,3},{4,12},{12,4},... | collective-permute-start | bytes 2359304 | tf_op jit(solution)/shard_map/ppermute | solution.py:435
  240.0 20.9 %copy-start.21 = (bf16[1024,1536]{1,0:T(8,128)(2,1)S(1)}, bf16[1024,1536]{1,0:T(8,128)(2,1)}, u32[]{:S(2)}) copy-start(bf16[1024,1536]{1,0:T(8,128)(2,1)} %copy-done.20) | copy-start | bytes 9437188
  259.0 3.8 copy-start.14
  261.0 1.8 copy-start.11
  261.2 17.0 %collective-permute-start.1 = (bf16[256,1536]{1,0:T(8,128)(2,1)S(1)}, bf16[256,1536]{1,0:T(8,128)(2,1)S(1)}, u32[]{:S(2)}, u32[]{:S(2)}) collective-permute-start(bf16[256,1536]{1,0:T(8,128)(2,1)S(1)} %fusion.42), channel_id=1, source_target_pairs={{0,8},{8,0},{1,9},{9,1},{2,10},{10,2},{3,11},{11,3},{4,12},{12,4},... | collective-permute-start | bytes 2359304 | tf_op jit(solution)/shard_map/ppermute | solution.py:435
  262.8 15.4 %copy-start.22 = (bf16[2,128,1536]{2,1,0:T(8,128)(2,1)S(1)}, bf16[2,128,1536]{2,1,0:T(8,128)(2,1)}, u32[]{:S(2)}) copy-start(bf16[2,128,1536]{2,1,0:T(8,128)(2,1)} %param.31) | copy-start | bytes 2359300
  264.6 16.8 %copy-start.26 = (bf16[384,1536]{1,0:T(8,128)(2,1)S(1)}, bf16[384,1536]{1,0:T(8,128)(2,1)}, u32[]{:S(2)}) copy-start(bf16[384,1536]{1,0:T(8,128)(2,1)} %wo_ref.1) | copy-start | bytes 3538948
  264.7 16.8 %copy-start.35 = (bf16[3,384,1536]{2,1,0:T(8,128)(2,1)S(1)}, bf16[3,384,1536]{2,1,0:T(8,128)(2,1)}, u32[]{:S(2)}) copy-start(bf16[3,384,1536]{2,1,0:T(8,128)(2,1)} %get-tuple-element.30) | copy-start | bytes 10616836
  281.4 2.3 copy-start.8
  281.4 2.3 copy-start.18
  288.1 7.8 slice-start
  290.5 5.3 slice-start.1
  295.8 1.6 copy-start.23
  297.4 1.8 copy-start.38
  299.2 2.7 copy-start.2
  303.4 1.4 copy-start.9
  303.4 1.6 copy-start.19
  303.4 187.9 %reduce-scatter.24.cloned.1.call-start = ((), (), s32[]{:S(2)}) async-start(), calls=%async_computation.13 | async-start | bytes 835584 | tf_op jit(solution)/shard_map/reduce_scatter | solution.py:553
  305.0 7.0 slice-start.2
  306.4 2.4 copy-start.3
  306.4 5.6 slice-start.3
  308.8 3.2 copy-start.24
  310.5 54.5 %collective-permute-start.7 = (bf16[2,384,1536]{2,1,0:T(8,128)(2,1)}, bf16[2,384,1536]{2,1,0:T(8,128)(2,1)}, u32[]{:S(2)}, u32[]{:S(2)}) collective-permute-start(bf16[2,384,1536]{2,1,0:T(8,128)(2,1)} %pad_maximum_fusion.1), channel_id=1, source_target_pairs={{0,16},{16,0},{1,17},{17,1},{2,18},{18,2},{3,19},{19,3},{4,20},{20... | collective-permute-start | bytes 7077896 | tf_op jit(solution)/shard_map/ppermute | solution.py:435
  318.2 5.6 copy-start.17
  323.8 1.4 copy-start.15
  325.2 2.2 copy-start.4
  327.4 16.3 %copy-start.28 = (f32[256,128]{1,0:T(8,128)S(1)}, f32[256,128]{1,0:T(8,128)}, u32[]{:S(2)}) copy-start(f32[256,128]{1,0:T(8,128)} %get-tuple-element.140.cos_ref) | copy-start | bytes 393220
  327.4 16.3 %copy-start.29 = (f32[256,128]{1,0:T(8,128)S(1)}, f32[256,128]{1,0:T(8,128)}, u32[]{:S(2)}) copy-start(f32[256,128]{1,0:T(8,128)} %get-tuple-element.98) | copy-start | bytes 393220
  329.1 100.2 %collective-permute-start.4 = (bf16[2,1536,384]{1,2,0:T(8,128)(2,1)}, bf16[2,1536,384]{1,2,0:T(8,128)(2,1)}, u32[]{:S(2)}, u32[]{:S(2)}) collective-permute-start(bf16[2,1536,384]{1,2,0:T(8,128)(2,1)} %pad_maximum_fusion), channel_id=1, source_target_pairs={{0,16},{16,0},{1,17},{17,1},{2,18},{18,2},{3,19},{19,3},{4,20},{20... | collective-permute-start | bytes 7077896 | tf_op jit(solution)/shard_map/ppermute | solution.py:435
  344.5 83.3 %collective-permute-start.6 = (bf16[1536,256]{0,1:T(8,128)(2,1)S(1)}, bf16[1536,256]{0,1:T(8,128)(2,1)S(1)}, u32[]{:S(2)}, u32[]{:S(2)}) collective-permute-start(bf16[1536,256]{0,1:T(8,128)(2,1)S(1)} %slice_bitcast_fusion.12), channel_id=1, source_target_pairs={{0,16},{16,0},{1,17},{17,1},{2,18},{18,2},{3,19},{19,3},{4,20},{20... | collective-permute-start | bytes 2359304 | tf_op jit(solution)/shard_map/ppermute | solution.py:435
  367.3 2.1 copy-start.5
  372.1 61.8 %collective-permute-start.8 = (bf16[384,1536]{1,0:T(8,128)(2,1)}, bf16[384,1536]{1,0:T(8,128)(2,1)}, u32[]{:S(2)}, u32[]{:S(2)}) collective-permute-start(bf16[384,1536]{1,0:T(8,128)(2,1)} %fusion.55), channel_id=1, source_target_pairs={{0,8},{8,0},{1,9},{9,1},{2,10},{10,2},{3,11},{11,3},{4,12},{12,4},... | collective-permute-start | bytes 3538952 | tf_op jit(solution)/shard_map/ppermute | solution.py:435
  429.2 179.0 %reduce-scatter.26.cloned.1.call-start = ((), (), s32[]{:S(2)}) async-start(), calls=%async_computation.14 | async-start | bytes 1327104
  429.3 4.6 copy-start.6
  437.5 172.5 %reduce-scatter.22.cloned.1.call-start = ((), (), s32[]{:S(2)}) async-start(), calls=%async_computation.12 | async-start | bytes 1327104
  437.8 28.2 %copy-start.7 = (f32[2,1536,384]{1,2,0:T(8,128)S(1)}, f32[2,1536,384]{1,2,0:T(8,128)}, u32[]{:S(2)}) copy-start(f32[2,1536,384]{1,2,0:T(8,128)} %convert_element_type.243) | copy-start | bytes 14155780
  440.3 25.7 %collective-permute-start.5 = (bf16[1536,384]{0,1:T(8,128)(2,1)S(1)}, bf16[1536,384]{0,1:T(8,128)(2,1)S(1)}, u32[]{:S(2)}, u32[]{:S(2)}) collective-permute-start(bf16[1536,384]{0,1:T(8,128)(2,1)S(1)} %fusion.54), channel_id=1, source_target_pairs={{0,8},{8,0},{1,9},{9,1},{2,10},{10,2},{3,11},{11,3},{4,12},{12,4},... | collective-permute-start | bytes 3538952 | tf_op jit(solution)/shard_map/ppermute | solution.py:435
  469.3 142.7 %all-gather.3.cloned.1.call-start = ((), (), s32[]{:S(2)}) async-start(), calls=%async_computation.11 | async-start | bytes 2359296 | tf_op jit(solution)/shard_map/all_gather | solution.py:555
  518.9 150.0 %reduce-scatter.16.cloned.1.call-start = ((), (), s32[]{:S(2)}) async-start(), calls=%async_computation.8 | async-start | bytes 7962624 | tf_op jit(solution)/shard_map/reduce_scatter | solution.py:573
  531.3 215.6 %reduce-scatter.18.cloned.1.call-start = ((), (), s32[]{:S(2)}) async-start(), calls=%async_computation.9 | async-start | bytes 7962624 | tf_op jit(solution)/shard_map/reduce_scatter | solution.py:573
  543.8 281.2 %reduce-scatter.20.cloned.1.call-start = ((), (), s32[]{:S(2)}) async-start(), calls=%async_computation.10 | async-start | bytes 7962624 | tf_op jit(solution)/shard_map/reduce_scatter | solution.py:573
  557.6 2.8 copy-start.16
  558.2 2.1 copy-start.27
  668.9 158.6 %copy-start.1 = (s32[8,1024]{1,0:T(8,128)S(1)}, s32[8,1024]{1,0:T(8,128)}, u32[]{:S(2)}) copy-start(s32[8,1024]{1,0:T(8,128)} %param.29) | copy-start | bytes 98308
  (3 other events, 2.7 us)
Sparse Core Ops, SparseCore 0:
  303.5 39.0 reduce-scatter.13
  429.3 61.9 reduce-scatter.23
  494.3 32.9 reduce-scatter.25
  530.1 32.0 reduce-scatter.21
  563.6 25.8 all-gather.2
  591.8 77.0 reduce-scatter.15
  671.3 75.5 reduce-scatter.17
  749.3 75.5 reduce-scatter.19
